TPU v7x, 128 devices: a whole 4x4x4 slice. The times are simulated.
128 devices in a mesh: view: 32 (over x, y, core), row: 4 (over z).
Axes of the slice: x: 4, y: 4, z: 4, core: 2. Of those that a mesh axis runs over, the one named last changes fastest.
Arguments:
- views_x: bfloat16 [32, 2048, 512], P('view', 'row'), may hold values from -17 to 17
- dy: bfloat16 [32, 2048, 512], P('view', 'row'), may hold values from -6 to 6
- w_query: bfloat16 [512, 512], replicated, may hold values from -0.25 to 0.25
- w_key: bfloat16 [512, 512], replicated, may hold values from -0.25 to 0.25
- w_value: bfloat16 [512, 512], replicated, may hold values from -0.25 to 0.25
- w_out: bfloat16 [512, 512], replicated, may hold values from -0.25 to 0.25
- key_lists: int32 [512, 32], replicated, may hold values from 0 to 2047, as said below
- key_counts: int32 [512], replicated, may hold values from 2 to 32
Outputs:
- grad_x: bfloat16 [32, 2048, 512], P('view', 'row')
- grad_w_out: float32 [512, 512], replicated
Inputs may be any that keep to these rules, and one draw needn't show every extreme that they name: `key_lists`: entry j of query block b names a key segment for j < key_counts[b] and is 0 from there on. The live entries of one list differ, and all lie in views other than the query block's. All query blocks of one device (its 4 blocks) name at most one segment of any one device (a device holds 16 segments).
All inputs are finite; a program needn't handle non-finite values.
Results may differ from a plain program's by a relative error of at most 0.03.
The roundings to bfloat16 on the way count: a program that leaves them out, or rounds other values in their place, can miss the bound.
Values may be sent and summed in bfloat16 or wider, within the bound.
No kernel may reach another device: no remote copies, remote signals or barrier semaphores. Data moves between devices by JAX's collectives and lax.ppermute only.
A program may use at most 128 MiB of HBM per device.

v0:
```python
import functools

import jax
import jax.numpy as jnp
from jax import lax
from jax.experimental import pallas as pl
from jax.experimental.pallas import tpu as pltpu
from jax.sharding import PartitionSpec as P

HEADS = 8
HEAD_DIM = 64
QUERY_BLOCK = 128
KEY_SEG = 32
MAXK = 32
AXES = ("view", "row")
SPAN = MAXK * KEY_SEG
CHUNK = 256
PAIR = 2 * HEAD_DIM
MIB = 1024 * 1024
F32 = jnp.float32
BF16 = jnp.bfloat16


def dot(a, b, ca=1, cb=0):
    return lax.dot_general(a, b, (((ca,), (cb,)), ((), ())), preferred_element_type=F32)


def gather_kernel(wanted, x_ref, out_ref):
    def step(i, carry):
        out_ref[i] = x_ref[jnp.maximum(wanted[i], 0)]
        return carry

    lax.fori_loop(0, out_ref.shape[0], step, 0, unroll=8)


def combine_kernel(wanted, back_ref, base_ref, out_ref, acc_ref):
    acc_ref[...] = base_ref[...]

    def step(i, carry):
        seg = wanted[i]

        @pl.when(seg >= 0)
        def _():
            acc_ref[seg] += back_ref[i].astype(F32)

        return carry

    lax.fori_loop(0, back_ref.shape[0], step, 0, unroll=4)
    out_ref[...] = acc_ref[...].astype(out_ref.dtype)


def attention_kernel(
    sources, counts, x_ref, q_ref, g_ref, gt_ref, wk_ref, wv_ref,
    ret_ref, att_ref, dq_ref,
    xg, ks, vs, ss, ps, ds, dk, dv, acc,
):
    blocks = q_ref.shape[0] // QUERY_BLOCK
    width = x_ref.shape[-1]
    pairs = width // PAIR
    acc[...] = jnp.zeros_like(acc)
    lane = lax.broadcasted_iota(jnp.int32, (QUERY_BLOCK, PAIR), 1)
    low_half = lane < HEAD_DIM
    row_ids = lax.broadcasted_iota(jnp.int32, (CHUNK, 2 * QUERY_BLOCK), 0)
    chunks = SPAN // CHUNK

    def split_heads(rows):
        zero = jnp.zeros_like(rows)
        return jnp.concatenate(
            [jnp.where(low_half, rows, zero), jnp.where(low_half, zero, rows)], axis=0
        )

    def fold(rows, op):
        return op(rows.reshape(CHUNK // 8, 8, rows.shape[-1]), axis=0)

    def block_step(b, carry):
        tok = pl.ds(pl.multiple_of(b * QUERY_BLOCK, QUERY_BLOCK), QUERY_BLOCK)
        live_rows = counts[b] * KEY_SEG
        for j in range(MAXK):
            xg[pl.ds(j * KEY_SEG, KEY_SEG), :] = x_ref[sources[b * MAXK + j]]
        for c in range(chunks):
            rows = pl.ds(c * CHUNK, CHUNK)
            part = xg[rows, :]
            ks[rows, :] = dot(part, wk_ref[...]).astype(BF16)
            vs[rows, :] = dot(part, wv_ref[...]).astype(BF16)
        for p in range(pairs):
            cols = pl.ds(p * PAIR, PAIR)
            qb = split_heads(q_ref[tok, cols])
            gb = split_heads(g_ref[tok, cols])
            top = jnp.full((8, 2 * QUERY_BLOCK), -1e30, F32)
            for c in range(chunks):
                rows = pl.ds(c * CHUNK, CHUNK)
                s = dot(ks[rows, cols], qb, 1, 1)
                s = jnp.where(row_ids < live_rows - c * CHUNK, s, F32(-1e30))
                ss[rows, :] = s
                top = jnp.maximum(top, fold(s, jnp.max))
            top = jnp.max(top, axis=0, keepdims=True)
            total = jnp.zeros((8, 2 * QUERY_BLOCK), F32)
            for c in range(chunks):
                rows = pl.ds(c * CHUNK, CHUNK)
                e = jnp.exp(ss[rows, :] - top)
                ss[rows, :] = e
                total = total + fold(e, jnp.sum)
            inverse = 1.0 / jnp.sum(total, axis=0, keepdims=True)
            for c in range(chunks):
                rows = pl.ds(c * CHUNK, CHUNK)
                w = ss[rows, :] * inverse
                ss[rows, :] = w
                low = w.astype(BF16)
                ps[rows, :] = low
                dv[rows, cols] = dot(low, gb).astype(BF16)
            att = dot(vs[:, cols], ps[...], 0, 0)
            deltas = []
            for h in range(2):
                here = att[h * HEAD_DIM:(h + 1) * HEAD_DIM, h * QUERY_BLOCK:(h + 1) * QUERY_BLOCK]
                here = here.astype(BF16)
                chan = pl.ds(p * PAIR + h * HEAD_DIM, HEAD_DIM)
                att_ref[chan, tok] = here
                both = here.astype(F32) * gt_ref[chan, tok].astype(F32)
                deltas.append(jnp.sum(both, axis=0, keepdims=True))
            delta = jnp.concatenate(deltas, axis=1)
            for c in range(chunks):
                rows = pl.ds(c * CHUNK, CHUNK)
                dp = dot(vs[rows, cols], gb, 1, 1)
                low = (ss[rows, :] * (dp - delta)).astype(BF16)
                ds[rows, :] = low
                dk[rows, cols] = dot(low, qb).astype(BF16)
            dq = dot(ks[:, cols], ds[...], 0, 0) * F32(HEAD_DIM ** -0.5)
            for h in range(2):
                here = dq[h * HEAD_DIM:(h + 1) * HEAD_DIM, h * QUERY_BLOCK:(h + 1) * QUERY_BLOCK]
                dq_ref[pl.ds(p * PAIR + h * HEAD_DIM, HEAD_DIM), tok] = here.astype(BF16)
        for c in range(chunks):
            rows = pl.ds(c * CHUNK, CHUNK)
            term = dot(dk[rows, :], wk_ref[...], 1, 1) + dot(dv[rows, :], wv_ref[...], 1, 1)
            per = CHUNK // KEY_SEG
            for j in range(per):
                acc[sources[b * MAXK + c * per + j]] += term[j * KEY_SEG:(j + 1) * KEY_SEG, :]
        return carry

    lax.fori_loop(0, blocks, block_step, 0)
    ret_ref[...] = acc[...].astype(BF16)


VMEM = pl.BlockSpec(memory_space=pltpu.VMEM)
SMEM = pl.BlockSpec(memory_space=pltpu.SMEM)


def exchange(v):
    return lax.all_to_all(v, AXES, split_axis=0, concat_axis=0, tiled=True)


def local(views_x, dy, w_query, w_key, w_value, w_out, key_lists, key_counts):
    width = views_x.shape[-1]
    x = views_x.reshape(-1, width)
    grads = dy.reshape(-1, width)
    tokens = x.shape[0]
    devices = lax.axis_size(AXES)
    me = lax.axis_index(AXES)
    seg_dev = tokens // KEY_SEG
    blocks = tokens // QUERY_BLOCK
    columns = jnp.arange(MAXK, dtype=jnp.int32)
    live = columns[None, :] < key_counts[:, None]
    asked = live & (key_lists // seg_dev == me)
    wanted = jnp.max(
        jnp.where(asked, key_lists % seg_dev, -1).reshape(devices, blocks * MAXK), axis=1
    )
    outgoing = pl.pallas_call(
        gather_kernel,
        out_shape=jax.ShapeDtypeStruct((devices, KEY_SEG, width), BF16),
        in_specs=[SMEM, VMEM],
        out_specs=VMEM,
        compiler_params=pltpu.CompilerParams(vmem_limit_bytes=16 * MIB),
        name="gather",
    )(wanted, x.reshape(seg_dev, KEY_SEG, width))
    fetched = exchange(outgoing)

    queries = dot(x, w_query).astype(BF16) * BF16(HEAD_DIM ** -0.5)
    grad_out = dot(grads, w_out, 1, 1).astype(BF16)
    grad_out_t = grad_out.T
    sources = lax.dynamic_slice_in_dim(key_lists, me * blocks, blocks, 0).reshape(-1) // seg_dev
    counts = lax.dynamic_slice_in_dim(key_counts, me * blocks, blocks, 0)
    pair2 = 2 * QUERY_BLOCK
    ret, att_t, dq_t = pl.pallas_call(
        attention_kernel,
        out_shape=[
            jax.ShapeDtypeStruct((devices, KEY_SEG, width), BF16),
            jax.ShapeDtypeStruct((width, tokens), BF16),
            jax.ShapeDtypeStruct((width, tokens), BF16),
        ],
        in_specs=[SMEM, SMEM] + [VMEM] * 6,
        out_specs=[VMEM] * 3,
        scratch_shapes=[
            pltpu.VMEM((SPAN, width), BF16),
            pltpu.VMEM((SPAN, width), BF16),
            pltpu.VMEM((SPAN, width), BF16),
            pltpu.VMEM((SPAN, pair2), F32),
            pltpu.VMEM((SPAN, pair2), BF16),
            pltpu.VMEM((SPAN, pair2), BF16),
            pltpu.VMEM((SPAN, width), BF16),
            pltpu.VMEM((SPAN, width), BF16),
            pltpu.VMEM((devices, KEY_SEG, width), F32),
        ],
        compiler_params=pltpu.CompilerParams(vmem_limit_bytes=48 * MIB),
        name="attention",
    )(sources, counts, fetched, queries, grad_out, grad_out_t, w_key, w_value)

    local_grad = dot(att_t, grads).astype(BF16)
    part = exchange(local_grad.reshape(devices, width // devices, width))
    part = jnp.sum(part.astype(F32), axis=0)
    grad_w_out = exchange(jnp.broadcast_to(part, (devices,) + part.shape)).reshape(width, width)

    back = exchange(ret)
    base = dot(dq_t, w_query, 0, 1)
    grad_x = pl.pallas_call(
        combine_kernel,
        out_shape=jax.ShapeDtypeStruct((seg_dev, KEY_SEG, width), BF16),
        in_specs=[SMEM, VMEM, VMEM],
        out_specs=VMEM,
        scratch_shapes=[pltpu.VMEM((seg_dev, KEY_SEG, width), F32)],
        compiler_params=pltpu.CompilerParams(vmem_limit_bytes=16 * MIB),
        name="combine",
    )(wanted, back, base.reshape(seg_dev, KEY_SEG, width))
    return grad_x.reshape(views_x.shape), grad_w_out


def solution(mesh):
    in_specs = (P("view", "row", None), P("view", "row", None), P(), P(), P(), P(), P(), P())
    out_specs = (P("view", "row", None), P())
    return jax.shard_map(local, mesh=mesh, in_specs=in_specs, out_specs=out_specs, check_vma=False)
```

profile of v0, /device:TPU:1, one launch (start us, length us, event | category | flops | bytes accessed | tf_op | source)
XLA Modules:
  0.0 212.2 jit_solution(4233474539089523734)
XLA Ops:
  0.7 1.0 fusion.6
  1.9 1.0 copy-done.2
  2.9 0.9 gather.1
  3.8 2.0 copy-done.1
  5.8 12.0 %all-to-all-start = ((bf16[128,32,512]{2,1,0:T(8,128)(2,1)}), bf16[128,32,512]{2,1,0:T(8,128)(2,1)}, u32[]{:S(2)}, u32[]{:S(2)}) async-start(bf16[128,32,512]{2,1,0:T(8,128)(2,1)} %copy-done.1), calls=%async_computation | async-start | bytes 8388608 | tf_op jit(solution)/shard_map/all_to_all | solution.py:148
  17.8 0.8 dynamic_slice.7.counts
  18.6 0.8 constant_dynamic-slice_fusion
  19.6 0.5 convolution_convert_fusion.1
  20.1 0.2 copy.15.g_ref
  20.3 2.3 %fusion.q_ref = bf16[512,512]{1,0:T(8,128)(2,1)} fusion(bf16[512,512]{1,0:T(8,128)(2,1)} %param.10, bf16[1,512,512]{2,1,0:T(8,128)(2,1)S(1)} %copy-done.3), kind=kOutput, calls=%fused_computation.3 | convolution fusion | flops 268959744 | bytes 1572864 | tf_op jit(solution)/shard_map/dot_general | solution.py:25
  22.6 48.1 %all-to-all-done.x_ref = bf16[128,32,512]{2,1,0:T(8,128)(2,1)} async-done(((bf16[128,32,512]{2,1,0:T(8,128)(2,1)}), bf16[128,32,512]{2,1,0:T(8,128)(2,1)}, u32[]{:S(2)}, u32[]{:S(2)}) %all-to-all-start) | async-done | bytes 4194336 | tf_op jit(solution)/shard_map/all_to_all | solution.py:148
  70.7 1.0 copy-done.6
  71.8 35.1 %attention.1 = (bf16[128,32,512]{2,1,0:T(8,128)(2,1)}, bf16[512,512]{1,0:T(8,128)(2,1)S(1)}, bf16[512,512]{1,0:T(8,128)(2,1)S(1)}) custom-call(s32[128]{0:T(128)S(1)} %and_select_fusion.sources, s32[4]{0:T(128)S(1)} %dynamic_slice.7.counts, bf16[128,32,512]{2,1,0:T(8,128)(2,1)} %all-to-all-done.x_ref, bf16[512,512]{1,0:T(8,128)(2,1)S(1)} %copy-done.6, ...), custom_call_target="tpu_custom_call" | custom-call | tf_op jit(solution)/shard_map/attention/pallas_call | solution.py:182
  106.9 0.8 copy-done.7
  107.7 0.4 convolution_convert_fusion
  108.2 17.3 %all_to_all.20 = bf16[128,4,512]{2,1,0:T(4,128)(2,1)S(1)} all-to-all(bf16[128,4,512]{2,1,0:T(4,128)(2,1)S(1)} %reshape.33), channel_id=1, replica_groups=mesh['view'=32,'row'=4] {'view','row'}, dimensions={0} | all-to-all | bytes 1048576 | tf_op jit(solution)/shard_map/all_to_all | solution.py:148
  125.6 0.3 convert_reduce_fusion
  125.8 0.1 broadcast_in_dim.4
  126.0 23.5 %all_to_all.21 = f32[128,4,512]{2,1,0:T(4,128)S(1)} all-to-all(f32[128,4,512]{2,1,0:T(4,128)S(1)} %broadcast_in_dim.4), channel_id=1, replica_groups=mesh['view'=32,'row'=4] {'view','row'}, dimensions={0} | all-to-all | bytes 2097152 | tf_op jit(solution)/shard_map/all_to_all | solution.py:148
  149.5 5.1 %all-to-all-start.1 = ((bf16[128,32,512]{2,1,0:T(8,128)(2,1)}), bf16[128,32,512]{2,1,0:T(8,128)(2,1)}, u32[]{:S(2)}, u32[]{:S(2)}) async-start(bf16[128,32,512]{2,1,0:T(8,128)(2,1)} %get-tuple-element.5), calls=%async_computation.1 | async-start | bytes 8388608 | tf_op jit(solution)/shard_map/all_to_all | solution.py:148
  154.6 1.5 fusion.10
  156.1 1.3 reshape.34
  157.4 50.2 %all-to-all-done.1.back_ref = bf16[128,32,512]{2,1,0:T(8,128)(2,1)} async-done(((bf16[128,32,512]{2,1,0:T(8,128)(2,1)}), bf16[128,32,512]{2,1,0:T(8,128)(2,1)}, u32[]{:S(2)}, u32[]{:S(2)}) %all-to-all-start.1) | async-done | bytes 4194336 | tf_op jit(solution)/shard_map/all_to_all | solution.py:148
  207.7 4.6 %combine.1 = bf16[16,32,512]{2,1,0:T(8,128)(2,1)} custom-call(s32[128]{0:T(128)S(1)} %reduce_max.18.wanted, bf16[128,32,512]{2,1,0:T(8,128)(2,1)} %all-to-all-done.1.back_ref, f32[16,32,512]{2,1,0:T(8,128)S(1)} %bitcast.18), custom_call_target="tpu_custom_call" | custom-call | tf_op jit(solution)/shard_map/combine/pallas_call | solution.py:213
  (22 shorter events, 0.6 us)
Async XLA Ops:
  0.6 19.0 %copy-start = (bf16[1,512,512]{2,1,0:T(8,128)(2,1)S(1)}, bf16[1,512,512]{2,1,0:T(8,128)(2,1)}, u32[]{:S(2)}) copy-start(bf16[1,512,512]{2,1,0:T(8,128)(2,1)} %param.9) | copy-start | bytes 1572868
  1.9 1.0 copy-start.2
  3.8 2.0 copy-start.1
  5.8 13.8 %copy-start.9 = (bf16[512,512]{1,0:T(8,128)(2,1)S(1)}, bf16[512,512]{1,0:T(8,128)(2,1)}, u32[]{:S(2)}) copy-start(bf16[512,512]{1,0:T(8,128)(2,1)} %param.13) | copy-start | bytes 1572868
  5.8 14.5 %copy-start.3 = (bf16[1,512,512]{2,1,0:T(8,128)(2,1)S(1)}, bf16[1,512,512]{2,1,0:T(8,128)(2,1)}, u32[]{:S(2)}) copy-start(bf16[1,512,512]{2,1,0:T(8,128)(2,1)} %param.8) | copy-start | bytes 1572868
  5.8 64.9 %all-to-all-start = ((bf16[128,32,512]{2,1,0:T(8,128)(2,1)}), bf16[128,32,512]{2,1,0:T(8,128)(2,1)}, u32[]{:S(2)}, u32[]{:S(2)}) async-start(bf16[128,32,512]{2,1,0:T(8,128)(2,1)} %copy-done.1), calls=%async_computation | async-start | bytes 8388608 | tf_op jit(solution)/shard_map/all_to_all | solution.py:148
  17.8 53.0 %copy-start.4 = (bf16[512,512]{1,0:T(8,128)(2,1)S(1)}, bf16[512,512]{1,0:T(8,128)(2,1)}, u32[]{:S(2)}) copy-start(bf16[512,512]{1,0:T(8,128)(2,1)} %wk_ref.1) | copy-start | bytes 1572868
  17.8 53.0 %copy-start.5 = (bf16[512,512]{1,0:T(8,128)(2,1)S(1)}, bf16[512,512]{1,0:T(8,128)(2,1)}, u32[]{:S(2)}) copy-start(bf16[512,512]{1,0:T(8,128)(2,1)} %wv_ref.1) | copy-start | bytes 1572868
  70.7 1.0 copy-start.6
  106.9 0.8 copy-start.7
  149.5 5.1 %copy-start.8 = (bf16[512,512]{1,0:T(8,128)(2,1)S(1)}, bf16[512,512]{1,0:T(8,128)(2,1)}, u32[]{:S(2)}) copy-start(bf16[512,512]{1,0:T(8,128)(2,1)} %copy-done.7) | copy-start | bytes 1572868
  149.5 58.2 %all-to-all-start.1 = ((bf16[128,32,512]{2,1,0:T(8,128)(2,1)}), bf16[128,32,512]{2,1,0:T(8,128)(2,1)}, u32[]{:S(2)}, u32[]{:S(2)}) async-start(bf16[128,32,512]{2,1,0:T(8,128)(2,1)} %get-tuple-element.5), calls=%async_computation.1 | async-start | bytes 8388608 | tf_op jit(solution)/shard_map/all_to_all | solution.py:148
where the time goes:
time: 213 us; the launch traced here: 212 us
  waiting for transfers between devices  98.3 us (46%)
  blocking collectives  40.8 us (19%)
  Pallas kernels  40.5 us (19%)
  starting transfers between devices  17 us (8%)
  local copies, waits for them, and re-layouts  8.58 us (4%)
  matrix products  4.73 us (2%)
    all_to_all x2, waiting for transfers between devices, exchange(): return lax.all_to_all(v, AXES, split_axis=0, concat_axis=0, tiled=True)  98.3 us
    all_to_all x2, blocking collectives, exchange(): return lax.all_to_all(v, AXES, split_axis=0, concat_axis=0, tiled=True)  40.8 us
    pallas_call x1, Pallas kernels, local(): pl.pallas_call(attention_kernel, out_shape=[jax.ShapeDtypeStruct((devices...  35.1 us
    all_to_all x2, starting transfers between devices, exchange(): return lax.all_to_all(v, AXES, split_axis=0, concat_axis=0, tiled=True)  17 us
    unnamed x20, local copies, waits for them, and re-layouts  4.87 us
    dot_general x4, matrix products, dot(): lax.dot_general(a, b, (((ca,), (cb,)), ((), ())), preferred_element_type=...  4.73 us
    pallas_call x1, Pallas kernels, local(): pl.pallas_call(combine_kernel, out_shape=jax.ShapeDtypeStruct((seg_dev, K...  4.55 us
  transfers between devices with their start and end apart: 2, of which 2 were waited for; matrix products, arithmetic and copies ran while one was open for 4% of the time, Pallas kernels for 0%

commit v1 on v0

v1 whole, which is shorter than its diff:
```python
import jax
import jax.numpy as jnp
from jax import lax
from jax.experimental import pallas as pl
from jax.experimental.pallas import tpu as pltpu
from jax.sharding import PartitionSpec as P

HEADS = 8
HEAD_DIM = 64
QUERY_BLOCK = 128
KEY_SEG = 32
MAXK = 32
AXES = ("view", "row")
SPAN = MAXK * KEY_SEG
CHUNK = 256
PAIR = 2 * HEAD_DIM
BOTH = 2 * QUERY_BLOCK
LANES = 128
MIB = 1024 * 1024
F32 = jnp.float32
BF16 = jnp.bfloat16


def dot(a, b, ca=1, cb=0):
    return lax.dot_general(a, b, (((ca,), (cb,)), ((), ())), preferred_element_type=F32)


def gather_kernel(wanted, x_ref, out_ref):
    def step(i, carry):
        out_ref[i] = x_ref[jnp.maximum(wanted[i], 0)]
        return carry

    lax.fori_loop(0, out_ref.shape[0], step, 0, unroll=8)


def combine_kernel(wanted, back_ref, base_ref, out_ref, acc_ref):
    acc_ref[...] = base_ref[...]

    def step(i, carry):
        seg = wanted[i]

        @pl.when(seg >= 0)
        def _():
            acc_ref[seg] += back_ref[i].astype(F32)

        return carry

    lax.fori_loop(0, back_ref.shape[0], step, 0, unroll=4)
    out_ref[...] = acc_ref[...].astype(out_ref.dtype)


def split_heads(rows):
    low_half = lax.broadcasted_iota(jnp.int32, rows.shape, 1) < HEAD_DIM
    zero = jnp.zeros_like(rows)
    return jnp.concatenate(
        [jnp.where(low_half, rows, zero), jnp.where(low_half, zero, rows)], axis=0
    )


def fold(rows, op):
    return op(rows.reshape(rows.shape[0] // 8, 8, rows.shape[-1]), axis=0)


def token_rows(b):
    return pl.ds(pl.multiple_of(b * QUERY_BLOCK, QUERY_BLOCK), QUERY_BLOCK)


def masked_scores(k_rows, qb, live_rows, start):
    s = dot(k_rows, qb, 1, 1)
    ids = lax.broadcasted_iota(jnp.int32, s.shape, 0)
    return jnp.where(ids < live_rows - start, s, F32(-1e30))


def forward_kernel(
    sources, counts, x_ref, q_ref, gt_ref, wk_ref, wv_ref, dy_ref,
    k_ref, v_ref, stat_ref, grad_ref,
    xg, ss, ps, att, sems,
):
    blocks = q_ref.shape[0] // QUERY_BLOCK
    width = x_ref.shape[-1]
    pairs = width // PAIR

    def fetch(b):
        def one(j, carry):
            pltpu.make_async_copy(
                x_ref.at[sources[b * MAXK + j]], xg.at[b * MAXK + j], sems.at[b]
            ).start()
            return carry

        lax.fori_loop(0, MAXK, one, 0, unroll=8)

    fetch(0)

    def block_step(b, carry):
        @pl.when(b + 1 < blocks)
        def _():
            fetch(b + 1)

        mine = xg.at[pl.ds(b * MAXK, MAXK)]
        pltpu.make_async_copy(mine, mine, sems.at[b]).wait()
        tok = token_rows(b)
        live_rows = counts[b] * KEY_SEG
        base = pl.multiple_of(b * SPAN, SPAN)
        segs = CHUNK // KEY_SEG
        for c in range(SPAN // CHUNK):
            rows = pl.ds(base + c * CHUNK, CHUNK)
            part = xg[pl.ds(b * MAXK + c * segs, segs)].reshape(CHUNK, width)
            k_ref[rows, :] = dot(part, wk_ref[...]).astype(BF16)
            v_ref[rows, :] = dot(part, wv_ref[...]).astype(BF16)
        for p in range(pairs):
            cols = pl.ds(p * PAIR, PAIR)
            qb = split_heads(q_ref[tok, cols])
            top = jnp.full((8, BOTH), -1e30, F32)
            for c in range(SPAN // CHUNK):
                rows = pl.ds(c * CHUNK, CHUNK)
                s = masked_scores(
                    k_ref[pl.ds(base + c * CHUNK, CHUNK), cols], qb, live_rows, c * CHUNK
                )
                ss[p % 2, rows, :] = s
                top = jnp.maximum(top, fold(s, jnp.max))
            top = jnp.max(top, axis=0, keepdims=True)
            total = jnp.zeros((8, BOTH), F32)
            for c in range(SPAN // CHUNK):
                rows = pl.ds(c * CHUNK, CHUNK)
                e = jnp.exp(ss[p % 2, rows, :] - top)
                ss[p % 2, rows, :] = e
                total = total + fold(e, jnp.sum)
            total = jnp.sum(total, axis=0, keepdims=True)
            inverse = 1.0 / total
            for c in range(SPAN // CHUNK):
                rows = pl.ds(c * CHUNK, CHUNK)
                ps[p % 2, rows, :] = (ss[p % 2, rows, :] * inverse).astype(BF16)
            out = dot(v_ref[pl.ds(base, SPAN), cols], ps[p % 2], 0, 0)
            deltas = []
            for h in range(2):
                here = out[h * HEAD_DIM:(h + 1) * HEAD_DIM, h * QUERY_BLOCK:(h + 1) * QUERY_BLOCK]
                here = here.astype(BF16)
                chan = pl.ds(p * PAIR + h * HEAD_DIM, HEAD_DIM)
                att[chan, tok] = here
                both = here.astype(F32) * gt_ref[chan, tok].astype(F32)
                deltas.append(jnp.sum(both, axis=0, keepdims=True))
            stat_ref[b, pl.ds(p, 1), :] = top + jnp.log(total)
            stat_ref[b, pl.ds(pairs + p, 1), :] = jnp.concatenate(deltas, axis=1)
        return carry

    lax.fori_loop(0, blocks, block_step, 0)
    per = grad_ref.shape[1]
    slots = width // LANES
    for r in range(width // 128):
        g = dot(att[pl.ds(r * 128, 128), :], dy_ref[...]).astype(BF16)
        for i in range(128 // per):
            for t in range(slots):
                grad_ref[(r * (128 // per) + i) * slots + t] = g[
                    i * per:(i + 1) * per, t * LANES:(t + 1) * LANES
                ]


def backward_kernel(
    sources, counts, k_ref, v_ref, q_ref, g_ref, stat_ref, wk_ref, wv_ref,
    ret_ref, dq_ref,
    ds, dk, dv, acc,
):
    blocks = q_ref.shape[0] // QUERY_BLOCK
    width = wk_ref.shape[-1]
    pairs = width // PAIR
    segs = CHUNK // KEY_SEG
    acc[...] = jnp.zeros_like(acc)

    def block_step(b, carry):
        tok = token_rows(b)
        live_rows = counts[b] * KEY_SEG
        base = pl.multiple_of(b * SPAN, SPAN)
        for p in range(pairs):
            cols = pl.ds(p * PAIR, PAIR)
            qb = split_heads(q_ref[tok, cols])
            gb = split_heads(g_ref[tok, cols])
            lse = stat_ref[b, pl.ds(p, 1), :]
            delta = stat_ref[b, pl.ds(pairs + p, 1), :]
            for c in range(SPAN // CHUNK):
                rows = pl.ds(c * CHUNK, CHUNK)
                there = pl.ds(base + c * CHUNK, CHUNK)
                s = masked_scores(k_ref[there, cols], qb, live_rows, c * CHUNK)
                w = jnp.exp(s - lse)
                dv[rows, cols] = dot(w.astype(BF16), gb).astype(BF16)
                dp = dot(v_ref[there, cols], gb, 1, 1)
                low = (w * (dp - delta)).astype(BF16)
                ds[p % 2, rows, :] = low
                dk[rows, cols] = dot(low, qb).astype(BF16)
            dq = dot(k_ref[pl.ds(base, SPAN), cols], ds[p % 2], 0, 0) * F32(HEAD_DIM ** -0.5)
            for h in range(2):
                here = dq[h * HEAD_DIM:(h + 1) * HEAD_DIM, h * QUERY_BLOCK:(h + 1) * QUERY_BLOCK]
                dq_ref[pl.ds(p * PAIR + h * HEAD_DIM, HEAD_DIM), tok] = here.astype(BF16)
        for c in range(SPAN // CHUNK):
            rows = pl.ds(c * CHUNK, CHUNK)
            term = dot(dk[rows, :], wk_ref[...], 1, 1) + dot(dv[rows, :], wv_ref[...], 1, 1)
            for j in range(segs):
                acc[sources[b * MAXK + c * segs + j]] += term[j * KEY_SEG:(j + 1) * KEY_SEG, :]
        return carry

    lax.fori_loop(0, blocks, block_step, 0)
    ret_ref[...] = acc[...].astype(BF16)


VMEM = pl.BlockSpec(memory_space=pltpu.VMEM)
SMEM = pl.BlockSpec(memory_space=pltpu.SMEM)
ANY = pl.BlockSpec(memory_space=pl.ANY)


def exchange(v):
    return lax.all_to_all(v, AXES, split_axis=0, concat_axis=0, tiled=True)


def forward(sources, counts, fetched, queries, grad_out_t, w_key, w_value, grads):
    devices, _, width = fetched.shape
    tokens = queries.shape[0]
    blocks = tokens // QUERY_BLOCK
    keys = blocks * SPAN
    per = width * width // (devices * LANES)
    return pl.pallas_call(
        forward_kernel,
        out_shape=[
            jax.ShapeDtypeStruct((keys, width), BF16),
            jax.ShapeDtypeStruct((keys, width), BF16),
            jax.ShapeDtypeStruct((blocks, 2 * width // PAIR, BOTH), F32),
            jax.ShapeDtypeStruct((devices, per, LANES), BF16),
        ],
        in_specs=[SMEM, SMEM, ANY] + [VMEM] * 5,
        out_specs=[VMEM] * 4,
        scratch_shapes=[
            pltpu.VMEM((blocks * MAXK, KEY_SEG, width), BF16),
            pltpu.VMEM((2, SPAN, BOTH), F32),
            pltpu.VMEM((2, SPAN, BOTH), BF16),
            pltpu.VMEM((width, tokens), BF16),
            pltpu.SemaphoreType.DMA((blocks,)),
        ],
        compiler_params=pltpu.CompilerParams(vmem_limit_bytes=32 * MIB),
        cost_estimate=pl.CostEstimate(
            flops=10_000_000_000, bytes_accessed=8 * MIB, transcendentals=4 * MIB
        ),
        name="forward",
    )(sources, counts, fetched, queries, grad_out_t, w_key, w_value, grads)


def backward(sources, counts, keys, values, queries, grad_out, stats, w_key, w_value, devices):
    tokens, width = queries.shape
    return pl.pallas_call(
        backward_kernel,
        out_shape=[
            jax.ShapeDtypeStruct((devices, KEY_SEG, width), BF16),
            jax.ShapeDtypeStruct((width, tokens), BF16),
        ],
        in_specs=[SMEM, SMEM] + [VMEM] * 7,
        out_specs=[VMEM] * 2,
        scratch_shapes=[
            pltpu.VMEM((2, SPAN, BOTH), BF16),
            pltpu.VMEM((SPAN, width), BF16),
            pltpu.VMEM((SPAN, width), BF16),
            pltpu.VMEM((devices, KEY_SEG, width), F32),
        ],
        compiler_params=pltpu.CompilerParams(vmem_limit_bytes=32 * MIB),
        cost_estimate=pl.CostEstimate(
            flops=20_000_000_000, bytes_accessed=16 * MIB, transcendentals=4 * MIB
        ),
        name="backward",
    )(sources, counts, keys, values, queries, grad_out, stats, w_key, w_value)


def local(views_x, dy, w_query, w_key, w_value, w_out, key_lists, key_counts):
    width = views_x.shape[-1]
    x = views_x.reshape(-1, width)
    grads = dy.reshape(-1, width)
    tokens = x.shape[0]
    devices = lax.axis_size(AXES)
    me = lax.axis_index(AXES)
    seg_dev = tokens // KEY_SEG
    blocks = tokens // QUERY_BLOCK
    columns = jnp.arange(MAXK, dtype=jnp.int32)
    live = columns[None, :] < key_counts[:, None]
    asked = live & (key_lists // seg_dev == me)
    wanted = jnp.max(
        jnp.where(asked, key_lists % seg_dev, -1).reshape(devices, blocks * MAXK), axis=1
    )
    outgoing = pl.pallas_call(
        gather_kernel,
        out_shape=jax.ShapeDtypeStruct((devices, KEY_SEG, width), BF16),
        in_specs=[SMEM, VMEM],
        out_specs=VMEM,
        compiler_params=pltpu.CompilerParams(vmem_limit_bytes=16 * MIB),
        name="gather",
    )(wanted, x.reshape(seg_dev, KEY_SEG, width))
    fetched = exchange(outgoing)

    queries = dot(x, w_query).astype(BF16) * BF16(HEAD_DIM ** -0.5)
    grad_out = dot(grads, w_out, 1, 1).astype(BF16)
    grad_out_t = grad_out.T
    sources = lax.dynamic_slice_in_dim(key_lists, me * blocks, blocks, 0).reshape(-1) // seg_dev
    counts = lax.dynamic_slice_in_dim(key_counts, me * blocks, blocks, 0)
    keys, values, stats, pieces = forward(
        sources, counts, fetched, queries, grad_out_t, w_key, w_value, grads
    )
    parts = exchange(pieces)
    ret, dq_t = backward(
        sources, counts, keys, values, queries, grad_out, stats, w_key, w_value, devices
    )
    part = jnp.sum(parts.astype(F32), axis=0)
    whole = lax.all_gather(part, AXES, axis=0)
    rows = part.shape[0]
    slots = width // LANES
    grad_w_out = whole.reshape(width // rows, slots, rows, LANES).transpose(0, 2, 1, 3)
    grad_w_out = grad_w_out.reshape(width, width)

    back = exchange(ret)
    base = dot(dq_t, w_query, 0, 1)
    grad_x = pl.pallas_call(
        combine_kernel,
        out_shape=jax.ShapeDtypeStruct((seg_dev, KEY_SEG, width), BF16),
        in_specs=[SMEM, VMEM, VMEM],
        out_specs=VMEM,
        scratch_shapes=[pltpu.VMEM((seg_dev, KEY_SEG, width), F32)],
        compiler_params=pltpu.CompilerParams(vmem_limit_bytes=16 * MIB),
        name="combine",
    )(wanted, back, base.reshape(seg_dev, KEY_SEG, width))
    return grad_x.reshape(views_x.shape), grad_w_out


def solution(mesh):
    in_specs = (P("view", "row", None), P("view", "row", None), P(), P(), P(), P(), P(), P())
    out_specs = (P("view", "row", None), P())
    return jax.shard_map(local, mesh=mesh, in_specs=in_specs, out_specs=out_specs, check_vma=False)
```

time: 213 us -> 249 us (1.17)
  blocking collectives: 40.8 us -> 0 us
  waiting for transfers between devices: 98.3 us -> 138 us
  between operations: 0.78 us -> 14.2 us
  local copies, waits for them, and re-layouts: 8.58 us -> 21.2 us
  starting transfers between devices: 17 us -> 27.3 us
  matrix products: 4.73 us -> 2.19 us
    all_gather x0 -> x1, waiting for transfers between devices: none -> 89 us  [local(): whole = lax.all_gather(part, AXES, axis=0)]
    all_to_all x2 -> x3, waiting for transfers between devices: 98.3 us -> 49.2 us  [exchange(): return lax.all_to_all(v, AXES, split_axis=0, concat_axis=0, tiled=True)]
    all_to_all x2 -> x0, blocking collectives: 40.8 us -> none  [exchange(): return lax.all_to_all(v, AXES, split_axis=0, concat_axis=0, tiled=True)]
    unnamed x20 -> x31, local copies, waits for them, and re-layouts: 4.87 us -> 17.5 us
    all_to_all x2 -> x3, starting transfers between devices: 17 us -> 27.3 us  [exchange(): return lax.all_to_all(v, AXES, split_axis=0, concat_axis=0, tiled=True)]
    dot_general x4 -> x3, matrix products: 4.73 us -> 2.19 us  [dot(): lax.dot_general(a, b, (((ca,), (cb,)), ((), ())), preferred_element_type=...]
    pallas_call x1 -> x2, Pallas kernels: 35.1 us -> 36.6 us  [the longest x1 18.4 us: forward(): pl.pallas_call(forward_kernel, out_shape=[jax.ShapeDtypeStruct((keys, wid...]
  transfers between devices with their start and end apart: 2 -> 4, of which waited for: 2 -> 2; matrix products, arithmetic and copies ran while one was open for 4% -> 3% of each run, Pallas kernels for 0% -> 7%
where the time goes in v1:
time: 249 us; the launch traced here: 248 us
  waiting for transfers between devices  138 us (55%)
  Pallas kernels  42 us (17%)
  starting transfers between devices  27.3 us (11%)
  local copies, waits for them, and re-layouts  21.2 us (9%)
  between operations  14.2 us (6%)
  other arithmetic  2.88 us (1%)
    all_gather x1, waiting for transfers between devices, local(): whole = lax.all_gather(part, AXES, axis=0)  89 us
    all_to_all x3, waiting for transfers between devices, exchange(): return lax.all_to_all(v, AXES, split_axis=0, concat_axis=0, tiled=True)  49.2 us
    all_to_all x3, starting transfers between devices, exchange(): return lax.all_to_all(v, AXES, split_axis=0, concat_axis=0, tiled=True)  27.3 us
    pallas_call x1, Pallas kernels, forward(): pl.pallas_call(forward_kernel, out_shape=[jax.ShapeDtypeStruct((keys, wid...  18.4 us
    pallas_call x1, Pallas kernels, backward(): pl.pallas_call(backward_kernel, out_shape=[jax.ShapeDtypeStruct((devices,...  18.2 us
    unnamed x31, local copies, waits for them, and re-layouts  17.5 us
  transfers between devices with their start and end apart: 4, of which 2 were waited for; matrix products, arithmetic and copies ran while one was open for 3% of the time, Pallas kernels for 7%

profile of v1, /device:TPU:1, one launch (start us, length us, event | category | flops | bytes accessed | tf_op | source)
XLA Modules:
  0.0 248.1 jit_solution(8954974529604990023)
XLA Ops:
  7.2 1.0 fusion.4
  8.4 1.0 copy-done.3
  9.4 0.9 gather.1
  10.4 2.0 copy-done.1
  12.3 12.0 %all-to-all-start = ((bf16[128,32,512]{2,1,0:T(8,128)(2,1)}), bf16[128,32,512]{2,1,0:T(8,128)(2,1)}, u32[]{:S(2)}, u32[]{:S(2)}) async-start(bf16[128,32,512]{2,1,0:T(8,128)(2,1)} %copy-done.1), calls=%async_computation | async-start | bytes 8388608 | tf_op jit(solution)/shard_map/all_to_all | solution.py:210
  26.8 1.2 fusion.q_ref
  28.1 49.2 %all-to-all-done.x_ref = bf16[128,32,512]{2,1,0:T(8,128)(2,1)} async-done(((bf16[128,32,512]{2,1,0:T(8,128)(2,1)}), bf16[128,32,512]{2,1,0:T(8,128)(2,1)}, u32[]{:S(2)}, u32[]{:S(2)}) %all-to-all-start) | async-done | bytes 4194336 | tf_op jit(solution)/shard_map/all_to_all | solution.py:210
  77.3 1.0 copy-done.7
  78.3 1.0 copy-done.8
  79.4 18.4 %forward.1 = (bf16[4096,512]{1,0:T(8,128)(2,1)S(1)}, bf16[4096,512]{1,0:T(8,128)(2,1)S(1)}, f32[4,8,256]{2,1,0:T(8,128)S(1)}, bf16[128,16,128]{2,1,0:T(8,128)(2,1)}) custom-call(s32[128]{0:T(128)S(1)} %and_select_fusion.sources, s32[4]{0:T(128)S(1)} %dynamic_slice.7.counts, bf16[128,32,512]{2,1,0:T(8,128)(2,1)} %all-to-all-done.x_ref, ...), custom_call_target="tpu_custom_call" | custom-call | flops 10000000000 | bytes 8388608 | tf_op jit(solution)/shard_map/forward/pallas_call | solution.py:219
  97.7 2.0 copy-done.10
  99.7 2.0 copy-done.12
  101.7 5.0 %all-to-all-start.2 = ((bf16[128,16,128]{2,1,0:T(8,128)(2,1)}), bf16[128,16,128]{2,1,0:T(8,128)(2,1)}, u32[]{:S(2)}, u32[]{:S(2)}) async-start(bf16[128,16,128]{2,1,0:T(8,128)(2,1)} %get-tuple-element.13), calls=%async_computation.2 | async-start | bytes 1048576 | tf_op jit(solution)/shard_map/all_to_all | solution.py:210
  106.6 1.0 copy-done.9
  107.7 2.2 copy-done.11
  109.9 2.2 copy-done.13
  112.1 18.2 %backward.1 = (bf16[128,32,512]{2,1,0:T(8,128)(2,1)S(1)}, bf16[512,512]{1,0:T(8,128)(2,1)S(1)}) custom-call(s32[128]{0:T(128)S(1)} %and_select_fusion.sources, s32[4]{0:T(128)S(1)} %dynamic_slice.7.counts, bf16[4096,512]{1,0:T(8,128)(2,1)S(1)} %copy-done.11, bf16[4096,512]{1,0:T(8,128)(2,1)S(1)} %copy-done.13, bf16[512,512]{1,0:T(8,128)(2,1)S(1)} %copy-done.9, ...), custom_call_target="tpu_custom_call" | custom-call | flops 20000000000 | bytes 16777216 | tf_op jit(solution)/shard_map/backward/pallas_call | solution.py:246
  130.3 2.0 copy-done.2
  132.3 10.4 %all-to-all-start.1 = ((bf16[128,32,512]{2,1,0:T(8,128)(2,1)}), bf16[128,32,512]{2,1,0:T(8,128)(2,1)}, u32[]{:S(2)}, u32[]{:S(2)}) async-start(bf16[128,32,512]{2,1,0:T(8,128)(2,1)} %copy-done.2), calls=%async_computation.1 | async-start | bytes 8388608 | tf_op jit(solution)/shard_map/all_to_all | solution.py:210
  142.7 1.8 convert_reduce_fusion
  145.0 89.0 %all-gather.3.cloned.1.call-done = f32[2048,128]{1,0:T(8,128)} async-done(((f32[16,128]{1,0:T(8,128)}), f32[2048,128]{1,0:T(8,128)}) %all-gather.3.cloned.1.call-update) | async-done | bytes 1048592 | tf_op jit(solution)/shard_map/all_gather | solution.py:306
  234.0 1.6 copy.16
  235.7 1.0 copy.19
  236.7 4.5 %combine.1 = bf16[16,32,512]{2,1,0:T(8,128)(2,1)} custom-call(s32[128]{0:T(128)S(1)} %reduce_max.18.wanted, bf16[128,32,512]{2,1,0:T(8,128)(2,1)} %all-to-all-done.1.back_ref, f32[16,32,512]{2,1,0:T(8,128)S(1)} %bitcast.22), custom_call_target="tpu_custom_call" | custom-call | tf_op jit(solution)/shard_map/combine/pallas_call | solution.py:314
  (34 shorter events, 3.3 us)
Async XLA Ops:
  7.2 19.7 %copy-start = (bf16[512,512]{1,0:T(8,128)(2,1)S(1)}, bf16[512,512]{1,0:T(8,128)(2,1)}, u32[]{:S(2)}) copy-start(bf16[512,512]{1,0:T(8,128)(2,1)} %param.10) | copy-start | bytes 1572868
  8.4 1.0 copy-start.3
  10.4 2.0 copy-start.1
  12.3 13.8 %copy-start.5 = (bf16[1,512,512]{2,1,0:T(8,128)(2,1)S(1)}, bf16[1,512,512]{2,1,0:T(8,128)(2,1)}, u32[]{:S(2)}) copy-start(bf16[1,512,512]{2,1,0:T(8,128)(2,1)} %param.9) | copy-start | bytes 1572868
  12.3 13.8 %copy-start.14 = (bf16[512,512]{1,0:T(8,128)(2,1)S(1)}, bf16[512,512]{1,0:T(8,128)(2,1)}, u32[]{:S(2)}) copy-start(bf16[512,512]{1,0:T(8,128)(2,1)} %param.13) | copy-start | bytes 1572868
  12.3 14.5 %copy-start.4 = (bf16[1,512,512]{2,1,0:T(8,128)(2,1)S(1)}, bf16[1,512,512]{2,1,0:T(8,128)(2,1)}, u32[]{:S(2)}) copy-start(bf16[1,512,512]{2,1,0:T(8,128)(2,1)} %param.8) | copy-start | bytes 1572868
  12.3 64.9 %all-to-all-start = ((bf16[128,32,512]{2,1,0:T(8,128)(2,1)}), bf16[128,32,512]{2,1,0:T(8,128)(2,1)}, u32[]{:S(2)}, u32[]{:S(2)}) async-start(bf16[128,32,512]{2,1,0:T(8,128)(2,1)} %copy-done.1), calls=%async_computation | async-start | bytes 8388608 | tf_op jit(solution)/shard_map/all_to_all | solution.py:210
  24.3 53.0 %copy-start.6 = (bf16[512,512]{1,0:T(8,128)(2,1)S(1)}, bf16[512,512]{1,0:T(8,128)(2,1)}, u32[]{:S(2)}) copy-start(bf16[512,512]{1,0:T(8,128)(2,1)} %wk_ref.3) | copy-start | bytes 1572868
  77.3 1.0 copy-start.7
  78.3 1.0 copy-start.8
  97.7 2.0 copy-start.10
  99.7 2.0 copy-start.12
  101.7 30.6 %all-to-all-start.2 = ((bf16[128,16,128]{2,1,0:T(8,128)(2,1)}), bf16[128,16,128]{2,1,0:T(8,128)(2,1)}, u32[]{:S(2)}, u32[]{:S(2)}) async-start(bf16[128,16,128]{2,1,0:T(8,128)(2,1)} %get-tuple-element.13), calls=%async_computation.2 | async-start | bytes 1048576 | tf_op jit(solution)/shard_map/all_to_all | solution.py:210
  106.6 1.0 copy-start.9
  107.7 2.2 copy-start.11
  109.9 2.2 copy-start.13
  130.3 2.0 copy-start.2
  132.3 104.4 %all-to-all-start.1 = ((bf16[128,32,512]{2,1,0:T(8,128)(2,1)}), bf16[128,32,512]{2,1,0:T(8,128)(2,1)}, u32[]{:S(2)}, u32[]{:S(2)}) async-start(bf16[128,32,512]{2,1,0:T(8,128)(2,1)} %copy-done.2), calls=%async_computation.1 | async-start | bytes 8388608 | tf_op jit(solution)/shard_map/all_to_all | solution.py:210
  142.6 91.4 %all-gather.3.cloned.1.call-start = ((), (), s32[]{:S(2)}) async-start(), calls=%async_computation.3 | async-start | bytes 1056768 | tf_op jit(solution)/shard_map/all_gather | solution.py:306
Sparse Core Ops, SparseCore 0:
  146.8 87.1 all-gather.2

commit v2 on v1

v2 whole, which is shorter than its diff:
```python
import jax
import jax.numpy as jnp
from jax import lax
from jax.experimental import pallas as pl
from jax.experimental.pallas import tpu as pltpu
from jax.sharding import PartitionSpec as P

HEAD_DIM = 64
QUERY_BLOCK = 128
KEY_SEG = 32
MAXK = 32
AXES = ("view", "row")
SPAN = MAXK * KEY_SEG
PAIR = 2 * HEAD_DIM
BOTH = 2 * QUERY_BLOCK
LANES = 128
MIB = 1024 * 1024
F32 = jnp.float32
BF16 = jnp.bfloat16
FC = 256
BC = 256
PC = 256
MXUMASK = False
NORM = False
ABL = ""

def dot(a, b, ca=1, cb=0):
    return lax.dot_general(a, b, (((ca,), (cb,)), ((), ())), preferred_element_type=F32)

def split_heads(rows):
    low_half = lax.broadcasted_iota(jnp.int32, rows.shape, 1) < HEAD_DIM
    zero = jnp.zeros_like(rows)
    return jnp.concatenate(
        [jnp.where(low_half, rows, zero), jnp.where(low_half, zero, rows)], axis=0)

def fold(rows, op):
    return op(rows.reshape(rows.shape[0] // 8, 8, rows.shape[-1]), axis=0)

def token_rows(b):
    return pl.ds(pl.multiple_of(b * QUERY_BLOCK, QUERY_BLOCK), QUERY_BLOCK)

def masked_scores(k_rows, qb, live_rows, start, bias=None):
    if MXUMASK:
        return dot(jnp.concatenate([k_rows, bias], axis=1), qb, 1, 1)
    s = dot(k_rows, qb, 1, 1)
    ids = lax.broadcasted_iota(jnp.int32, s.shape, 0)
    return jnp.where(ids < live_rows - start, s, F32(-1e30))

def with_ones(qb):
    if not MXUMASK:
        return qb
    lane = lax.broadcasted_iota(jnp.int32, (BOTH, LANES), 1)
    return jnp.concatenate([qb, jnp.where(lane == 0, 1.0, 0.0).astype(BF16)], axis=1)

def fill_bias(bias, live_rows):
    if MXUMASK:
        ids = lax.broadcasted_iota(jnp.int32, bias.shape, 0)
        lane = lax.broadcasted_iota(jnp.int32, bias.shape, 1)
        bias[...] = jnp.where((ids >= live_rows) & (lane == 0), F32(-1e30), F32(0)).astype(BF16)

def forward_kernel(
    sources, counts, x_hbm, q_hbm, gt_hbm, wk_hbm, wv_hbm, dy_hbm,
    k_out, v_out, stat_ref, grad_ref,
    xg, ks, vs, ss, ps, att, bias, q_ref, gt_ref, wk_ref, wv_ref, dy_ref, sems, osems, wsems,
):
    blocks = q_ref.shape[0] // QUERY_BLOCK
    width = x_hbm.shape[-1]
    pairs = width // PAIR

    def fetch(b):
        def one(j, carry):
            pltpu.make_async_copy(
                x_hbm.at[sources[b * MAXK + j]], xg.at[b * MAXK + j], sems.at[b]
            ).start()
            return carry
        lax.fori_loop(0, MAXK, one, 0, unroll=8)

    weights = [(wk_hbm, wk_ref), (wv_hbm, wv_ref), (q_hbm, q_ref), (gt_hbm, gt_ref), (dy_hbm, dy_ref)]
    loads = [pltpu.make_async_copy(a, z, wsems.at[i]) for i, (a, z) in enumerate(weights)]
    loads[0].start()
    loads[1].start()
    fetch(0)
    for load in loads[2:]:
        load.start()
    loads[0].wait()
    loads[1].wait()

    def block_step(b, carry):
        @pl.when(b + 1 < blocks)
        def _():
            fetch(b + 1)
        mine = xg.at[pl.ds(b * MAXK, MAXK)]
        pltpu.make_async_copy(mine, mine, sems.at[b]).wait()
        tok = token_rows(b)
        live_rows = counts[b] * KEY_SEG
        base = pl.multiple_of(b * SPAN, SPAN)
        segs = PC // KEY_SEG
        fill_bias(bias, live_rows)
        if "noproj" not in ABL:
            for c in range(SPAN // PC):
                rows = pl.ds(base + c * PC, PC)
                part = xg[pl.ds(b * MAXK + c * segs, segs)].reshape(PC, width)
                ks[rows, :] = dot(part, wk_ref[...]).astype(BF16)
                vs[rows, :] = dot(part, wv_ref[...]).astype(BF16)
        span = pl.ds(base, SPAN)
        pltpu.make_async_copy(ks.at[span], k_out.at[span], osems.at[0]).start()
        pltpu.make_async_copy(vs.at[span], v_out.at[span], osems.at[1]).start()

        @pl.when(b == 0)
        def _():
            for load in loads[2:]:
                load.wait()
        for p in range(pairs if "nopair" not in ABL else 0):
            cols = pl.ds(p * PAIR, PAIR)
            qb = with_ones(split_heads(q_ref[tok, cols]))
            top = jnp.full((8, BOTH), -1e30, F32)
            for c in range(SPAN // FC):
                rows = pl.ds(c * FC, FC)
                s = masked_scores(ks[pl.ds(base + c * FC, FC), cols], qb, live_rows, c * FC, bias[rows, :])
                ss[p % 2, rows, :] = s
                top = jnp.maximum(top, fold(s, jnp.max))
            top = jnp.max(top, axis=0, keepdims=True)
            total = jnp.zeros((8, BOTH), F32)
            for c in range(SPAN // FC):
                rows = pl.ds(c * FC, FC)
                e = jnp.exp(ss[p % 2, rows, :] - top)
                if NORM:
                    ss[p % 2, rows, :] = e
                else:
                    ps[p % 2, rows, :] = e.astype(BF16)
                total = total + fold(e, jnp.sum)
            total = jnp.sum(total, axis=0, keepdims=True)
            inverse = 1.0 / total
            if NORM:
                for c in range(SPAN // FC):
                    rows = pl.ds(c * FC, FC)
                    ps[p % 2, rows, :] = (ss[p % 2, rows, :] * inverse).astype(BF16)
            out = dot(vs[pl.ds(base, SPAN), cols], ps[p % 2], 0, 0)
            deltas = []
            for h in range(2):
                here = out[h * HEAD_DIM:(h + 1) * HEAD_DIM, h * QUERY_BLOCK:(h + 1) * QUERY_BLOCK]
                if not NORM:
                    here = here * inverse[:, h * QUERY_BLOCK:(h + 1) * QUERY_BLOCK]
                here = here.astype(BF16)
                chan = pl.ds(p * PAIR + h * HEAD_DIM, HEAD_DIM)
                att[chan, tok] = here
                both = here.astype(F32) * gt_ref[chan, tok].astype(F32)
                deltas.append(jnp.sum(both, axis=0, keepdims=True))
            stat_ref[b, pl.ds(p, 1), :] = top + jnp.log(total)
            stat_ref[b, pl.ds(pairs + p, 1), :] = jnp.concatenate(deltas, axis=1)
        return carry

    lax.fori_loop(0, blocks, block_step, 0)
    per = grad_ref.shape[1]
    slots = width // LANES
    for r in range(width // 128 if "nograd" not in ABL else 0):
        g = dot(att[pl.ds(r * 128, 128), :], dy_ref[...]).astype(BF16)
        for i in range(128 // per):
            for t in range(slots):
                grad_ref[(r * (128 // per) + i) * slots + t] = g[
                    i * per:(i + 1) * per, t * LANES:(t + 1) * LANES
                ]
    pltpu.make_async_copy(ks, k_out, osems.at[0]).wait()
    pltpu.make_async_copy(vs, v_out, osems.at[1]).wait()


def backward_kernel(
    sources, counts, k_hbm, v_hbm, q_hbm, g_hbm, stat_ref, wk_hbm, wv_hbm,
    ret_hbm, dq_ref,
    ks, vs, ds, dk, dv, acc, bias, q_ref, g_ref, wk_ref, wv_ref, out, sems, wsems, osem,
):
    blocks = q_ref.shape[0] // QUERY_BLOCK
    width = wk_ref.shape[-1]
    pairs = width // PAIR
    segs = PC // KEY_SEG
    devices = acc.shape[0]
    weights = [(q_hbm, q_ref), (g_hbm, g_ref), (wk_hbm, wk_ref), (wv_hbm, wv_ref)]
    loads = [pltpu.make_async_copy(a, z, wsems.at[i]) for i, (a, z) in enumerate(weights)]
    for load in loads[:2]:
        load.start()
    for b in range(blocks):
        span = pl.ds(b * SPAN, SPAN)
        pltpu.make_async_copy(k_hbm.at[span], ks.at[span], sems.at[b, 0]).start()
        pltpu.make_async_copy(v_hbm.at[span], vs.at[span], sems.at[b, 1]).start()
        if b == 0:
            for load in loads[2:]:
                load.start()
    acc[...] = jnp.zeros_like(acc)
    for load in loads:
        load.wait()

    def block_step(b, carry):
        tok = token_rows(b)
        live_rows = counts[b] * KEY_SEG
        base = pl.multiple_of(b * SPAN, SPAN)
        span = pl.ds(base, SPAN)
        fill_bias(bias, live_rows)
        pltpu.make_async_copy(ks.at[span], ks.at[span], sems.at[b, 0]).wait()
        pltpu.make_async_copy(vs.at[span], vs.at[span], sems.at[b, 1]).wait()
        for p in range(pairs if "nopair" not in ABL else 0):
            cols = pl.ds(p * PAIR, PAIR)
            qb = split_heads(q_ref[tok, cols])
            qo = with_ones(qb)
            gb = split_heads(g_ref[tok, cols])
            lse = stat_ref[b, pl.ds(p, 1), :]
            delta = stat_ref[b, pl.ds(pairs + p, 1), :]
            for c in range(SPAN // BC):
                rows = pl.ds(c * BC, BC)
                there = pl.ds(base + c * BC, BC)
                s = masked_scores(ks[there, cols], qo, live_rows, c * BC, bias[rows, :])
                w = jnp.exp(s - lse)
                dv[rows, cols] = dot(w.astype(BF16), gb).astype(BF16)
                dp = dot(vs[there, cols], gb, 1, 1)
                low = (w * (dp - delta)).astype(BF16)
                ds[p % 2, rows, :] = low
                dk[rows, cols] = dot(low, qb).astype(BF16)
            dq = dot(ks[pl.ds(base, SPAN), cols], ds[p % 2], 0, 0) * F32(HEAD_DIM ** -0.5)
            for h in range(2):
                here = dq[h * HEAD_DIM:(h + 1) * HEAD_DIM, h * QUERY_BLOCK:(h + 1) * QUERY_BLOCK]
                dq_ref[pl.ds(p * PAIR + h * HEAD_DIM, HEAD_DIM), tok] = here.astype(BF16)
        for c in range(SPAN // PC if "noproj" not in ABL else 0):
            rows = pl.ds(c * PC, PC)
            term = dot(dk[rows, :], wk_ref[...], 1, 1) + dot(dv[rows, :], wv_ref[...], 1, 1)
            for j in range(segs):
                acc[sources[b * MAXK + c * segs + j]] += term[j * KEY_SEG:(j + 1) * KEY_SEG, :]
        return carry

    lax.fori_loop(0, blocks, block_step, 0)
    groups = 4
    size = devices // groups
    for t in range(groups):
        part = pl.ds(t * size, size)
        for u in range(width // LANES):
            out[part, pl.ds(u * KEY_SEG, KEY_SEG), :] = acc[part, :, pl.ds(u * LANES, LANES)].astype(BF16)
        pltpu.make_async_copy(
            out.at[part], ret_hbm.at[part, pl.ds(0, KEY_SEG * width // LANES)], osem).start()
    pltpu.make_async_copy(out, ret_hbm.at[:, pl.ds(0, KEY_SEG * width // LANES)], osem).wait()


VMEM = pl.BlockSpec(memory_space=pltpu.VMEM)
SMEM = pl.BlockSpec(memory_space=pltpu.SMEM)
ANY = pl.BlockSpec(memory_space=pl.ANY)

def square(width, tokens):
    return pltpu.VMEM((tokens, width), BF16)

def forward(sources, counts, fetched, queries, grad_out_t, w_key, w_value, grads):
    devices, _, width = fetched.shape
    tokens = queries.shape[0]
    blocks = tokens // QUERY_BLOCK
    keys = blocks * SPAN
    per = width * width // (devices * LANES)
    return pl.pallas_call(
        forward_kernel,
        out_shape=[
            jax.ShapeDtypeStruct((keys, width), BF16),
            jax.ShapeDtypeStruct((keys, width), BF16),
            jax.ShapeDtypeStruct((blocks, 2 * width // PAIR, BOTH), F32),
            jax.ShapeDtypeStruct((devices, per, LANES), BF16),
        ],
        in_specs=[SMEM, SMEM] + [ANY] * 6,
        out_specs=[ANY, ANY, VMEM, VMEM],
        scratch_shapes=[
            pltpu.VMEM((blocks * MAXK, KEY_SEG, width), BF16),
            pltpu.VMEM((keys, width), BF16),
            pltpu.VMEM((keys, width), BF16),
            pltpu.VMEM((2, SPAN, BOTH), F32),
            pltpu.VMEM((2, SPAN, BOTH), BF16),
            pltpu.VMEM((width, tokens), BF16),
            pltpu.VMEM((SPAN, LANES), BF16),
            pltpu.VMEM((tokens, width), BF16),
            pltpu.VMEM((width, tokens), BF16),
            pltpu.VMEM((width, width), BF16),
            pltpu.VMEM((width, width), BF16),
            pltpu.VMEM((tokens, width), BF16),
            pltpu.SemaphoreType.DMA((blocks,)),
            pltpu.SemaphoreType.DMA((2,)),
            pltpu.SemaphoreType.DMA((5,)),
        ],
        compiler_params=pltpu.CompilerParams(vmem_limit_bytes=60 * MIB),
        cost_estimate=pl.CostEstimate(
            flops=10_000_000_000, bytes_accessed=8 * MIB, transcendentals=4 * MIB),
        name="forward",
    )(sources, counts, fetched, queries, grad_out_t, w_key, w_value, grads)


def backward(sources, counts, keys, values, queries, grad_out, stats, w_key, w_value, devices):
    tokens, width = queries.shape
    blocks = tokens // QUERY_BLOCK
    lines = KEY_SEG * width // LANES
    extra = width * width // (devices * LANES)
    return pl.pallas_call(
        backward_kernel,
        out_shape=[
            jax.ShapeDtypeStruct((devices, lines + extra, LANES), BF16),
            jax.ShapeDtypeStruct((width, tokens), BF16),
        ],
        in_specs=[SMEM, SMEM] + [ANY] * 4 + [VMEM] + [ANY] * 2,
        out_specs=[ANY, VMEM],
        scratch_shapes=[
            pltpu.VMEM((blocks * SPAN, width), BF16),
            pltpu.VMEM((blocks * SPAN, width), BF16),
            pltpu.VMEM((2, SPAN, BOTH), BF16),
            pltpu.VMEM((SPAN, width), BF16),
            pltpu.VMEM((SPAN, width), BF16),
            pltpu.VMEM((devices, KEY_SEG, width), F32),
            pltpu.VMEM((SPAN, LANES), BF16),
            pltpu.VMEM((tokens, width), BF16),
            pltpu.VMEM((tokens, width), BF16),
            pltpu.VMEM((width, width), BF16),
            pltpu.VMEM((width, width), BF16),
            pltpu.VMEM((devices, lines, LANES), BF16),
            pltpu.SemaphoreType.DMA((blocks, 2)),
            pltpu.SemaphoreType.DMA((4,)),
            pltpu.SemaphoreType.DMA,
        ],
        compiler_params=pltpu.CompilerParams(vmem_limit_bytes=60 * MIB),
        cost_estimate=pl.CostEstimate(
            flops=20_000_000_000, bytes_accessed=16 * MIB, transcendentals=4 * MIB),
        name="backward",
    )(sources, counts, keys, values, queries, grad_out, stats, w_key, w_value)


def gather_kernel(wanted, x_ref, out_ref, sem):
    def step(i, carry):
        pltpu.make_async_copy(x_ref.at[jnp.maximum(wanted[i], 0)], out_ref.at[i], sem).start()
        return carry

    lax.fori_loop(0, out_ref.shape[0], step, 0, unroll=8)
    pltpu.make_async_copy(out_ref, out_ref, sem).wait()


def finish_kernel(parts_ref, ret_in, ret_out, wide, sem):
    total = jnp.sum(parts_ref[...].astype(F32), axis=0)
    wide[...] = jnp.broadcast_to(total.astype(BF16)[None], wide.shape)
    extra = wide.shape[1]
    rows = pl.ds(ret_out.shape[1] - extra, extra)
    copy = pltpu.make_async_copy(wide, ret_out.at[:, rows], sem)
    copy.start()
    copy.wait()


def combine_kernel(wanted, back_hbm, base_ref, out_ref, grad_ref, back, acc, sems):
    devices, lines, _ = back.shape
    groups = sems.shape[0]
    size = devices // groups
    width = base_ref.shape[-1]
    slots = width // LANES
    extra = lines - KEY_SEG * slots

    def copy(t):
        part = pl.ds(t * size, size)
        return pltpu.make_async_copy(back_hbm.at[part], back.at[part], sems.at[t])

    for t in range(groups):
        copy(t).start()
    acc[...] = base_ref[...]
    for t in range(groups):
        copy(t).wait()

        def step(i, carry):
            seg = wanted[i]

            @pl.when(seg >= 0)
            def _():
                for u in range(slots):
                    cols = pl.ds(u * LANES, LANES)
                    acc[seg, :, cols] += back[i, pl.ds(u * KEY_SEG, KEY_SEG), :].astype(F32)

            return carry

        lax.fori_loop(t * size, (t + 1) * size, step, 0)
        for i in range(t * size, (t + 1) * size):
            rows = pl.ds((i // slots) * extra, extra)
            cols = pl.ds((i % slots) * LANES, LANES)
            grad_ref[rows, cols] = back[i, pl.ds(lines - extra, extra), :].astype(F32)
    out_ref[...] = acc[...].astype(out_ref.dtype)


def exchange(v):
    return lax.all_to_all(v, AXES, split_axis=0, concat_axis=0, tiled=True)


def local(views_x, dy, w_query, w_key, w_value, w_out, key_lists, key_counts):
    width = views_x.shape[-1]
    x = views_x.reshape(-1, width)
    grads = dy.reshape(-1, width)
    tokens = x.shape[0]
    devices = lax.axis_size(AXES)
    me = lax.axis_index(AXES)
    seg_dev = tokens // KEY_SEG
    blocks = tokens // QUERY_BLOCK
    columns = jnp.arange(MAXK, dtype=jnp.int32)
    live = columns[None, :] < key_counts[:, None]
    asked = live & (key_lists // seg_dev == me)
    wanted = jnp.max(
        jnp.where(asked, key_lists % seg_dev, -1).reshape(devices, blocks * MAXK), axis=1
    )
    outgoing = pl.pallas_call(
        gather_kernel,
        out_shape=jax.ShapeDtypeStruct((devices, KEY_SEG, width), BF16),
        in_specs=[SMEM, ANY],
        out_specs=ANY,
        scratch_shapes=[pltpu.SemaphoreType.DMA],
        name="gather",
    )(wanted, x.reshape(seg_dev, KEY_SEG, width))
    fetched = exchange(outgoing)

    queries = dot(x, w_query).astype(BF16) * BF16(HEAD_DIM ** -0.5)
    grad_out = dot(grads, w_out, 1, 1).astype(BF16)
    grad_out_t = grad_out.T
    sources = lax.dynamic_slice_in_dim(key_lists, me * blocks, blocks, 0).reshape(-1) // seg_dev
    counts = lax.dynamic_slice_in_dim(key_counts, me * blocks, blocks, 0)
    keys, values, stats, pieces = forward(
        sources, counts, fetched, queries, grad_out_t, w_key, w_value, grads
    )
    parts = exchange(pieces)
    ret, dq_t = backward(
        sources, counts, keys, values, queries, grad_out, stats, w_key, w_value, devices
    )
    ret = pl.pallas_call(
        finish_kernel,
        out_shape=jax.ShapeDtypeStruct(ret.shape, ret.dtype),
        in_specs=[VMEM, ANY],
        out_specs=ANY,
        scratch_shapes=[pltpu.VMEM(parts.shape, BF16), pltpu.SemaphoreType.DMA],
        input_output_aliases={1: 0},
        name="finish",
    )(parts, ret)
    back = exchange(ret)
    base = dot(dq_t, w_query, 0, 1)
    grad_x, grad_w_out = pl.pallas_call(
        combine_kernel,
        out_shape=[
            jax.ShapeDtypeStruct((seg_dev, KEY_SEG, width), BF16),
            jax.ShapeDtypeStruct((width, width), F32),
        ],
        in_specs=[SMEM, ANY, VMEM],
        out_specs=[VMEM, VMEM],
        scratch_shapes=[
            pltpu.VMEM(ret.shape, BF16),
            pltpu.VMEM((seg_dev, KEY_SEG, width), F32),
            pltpu.SemaphoreType.DMA((8,)),
        ],
        compiler_params=pltpu.CompilerParams(vmem_limit_bytes=24 * MIB),
        name="combine",
    )(wanted, back, base.reshape(seg_dev, KEY_SEG, width))
    return grad_x.reshape(views_x.shape), grad_w_out


def solution(mesh):
    in_specs = (P("view", "row", None), P("view", "row", None), P(), P(), P(), P(), P(), P())
    out_specs = (P("view", "row", None), P())
    return jax.shard_map(local, mesh=mesh, in_specs=in_specs, out_specs=out_specs, check_vma=False)
```

time: 249 us -> 321 us (1.29)
  Pallas kernels: 42 us -> 179 us
  waiting for transfers between devices: 138 us -> 106 us
  local copies, waits for them, and re-layouts: 21.2 us -> 4.23 us
  between operations: 14.2 us -> 0.81 us
    pallas_call x1, Pallas kernels: 0.91 us -> 129 us  [local(): pl.pallas_call(gather_kernel, out_shape=jax.ShapeDtypeStruct((devices, KE...]
    all_gather x1 -> x0, waiting for transfers between devices: 89 us -> none  [local(): whole = lax.all_gather(part, AXES, axis=0)]
    all_to_all x3, waiting for transfers between devices: 49.2 us -> 106 us  [exchange(): return lax.all_to_all(v, AXES, split_axis=0, concat_axis=0, tiled=True)]
    unnamed x31 -> x16, local copies, waits for them, and re-layouts: 17.5 us -> 0.83 us
    pallas_call x1, Pallas kernels: 18.2 us -> 24.1 us  [backward(): pl.pallas_call(backward_kernel, out_shape=[jax.ShapeDtypeStruct((devices,...]
    pallas_call x1 -> x2, Pallas kernels: 4.54 us -> 6.69 us  [the longest x1 4.63 us: local(): pl.pallas_call(combine_kernel, out_shape=[jax.ShapeDtypeStruct((seg_dev,...]
  transfers between devices with their start and end apart: 4 -> 3, of which waited for: 2 -> 2; matrix products, arithmetic and copies ran while one was open for 3% -> 2% of each run, Pallas kernels for 7% -> 8%
where the time goes in v2:
time: 321 us; the launch traced here: 320 us
  Pallas kernels  179 us (56%)
  waiting for transfers between devices  106 us (33%)
  starting transfers between devices  26.1 us (8%)
  local copies, waits for them, and re-layouts  4.23 us (1%)
    pallas_call x1, Pallas kernels, local(): pl.pallas_call(gather_kernel, out_shape=jax.ShapeDtypeStruct((devices, KE...  129 us
    all_to_all x3, waiting for transfers between devices, exchange(): return lax.all_to_all(v, AXES, split_axis=0, concat_axis=0, tiled=True)  106 us
    all_to_all x3, starting transfers between devices, exchange(): return lax.all_to_all(v, AXES, split_axis=0, concat_axis=0, tiled=True)  26.1 us
    pallas_call x1, Pallas kernels, backward(): pl.pallas_call(backward_kernel, out_shape=[jax.ShapeDtypeStruct((devices,...  24.1 us
    pallas_call x1, Pallas kernels, forward(): pl.pallas_call(forward_kernel, out_shape=[jax.ShapeDtypeStruct((keys, wid...  19.2 us
  transfers between devices with their start and end apart: 3, of which 2 were waited for; matrix products, arithmetic and copies ran while one was open for 2% of the time, Pallas kernels for 8%

profile of v2, /device:TPU:1, one launch (start us, length us, event | category | flops | bytes accessed | tf_op | source)
XLA Modules:
  0.0 320.0 jit_solution(929324760782022213)
XLA Ops:
  0.6 0.0 copy-start
  0.7 1.0 fusion.4
  1.6 0.1 reduce_max.14
  1.7 0.6 reduce_max.18.wanted
  2.4 128.8 %gather.1 = bf16[128,32,512]{2,1,0:T(8,128)(2,1)} custom-call(s32[128]{0:T(128)} %reduce_max.18.wanted, bf16[16,32,512]{2,1,0:T(8,128)(2,1)} %bitcast.16), custom_call_target="tpu_custom_call" | custom-call | tf_op jit(solution)/shard_map/gather/pallas_call | solution.py:399
  131.3 12.0 %all-to-all-start = ((bf16[128,32,512]{2,1,0:T(8,128)(2,1)}), bf16[128,32,512]{2,1,0:T(8,128)(2,1)}, u32[]{:S(2)}, u32[]{:S(2)}) async-start(bf16[128,32,512]{2,1,0:T(8,128)(2,1)} %gather.1), calls=%async_computation | async-start | bytes 8388608 | tf_op jit(solution)/shard_map/all_to_all | solution.py:381
  143.2 1.3 dynamic_slice.7.counts
  144.6 0.8 constant_dynamic-slice_fusion
  145.3 0.1 copy.13
  145.4 0.1 reshape.22
  145.5 0.5 convolution_convert_fusion.g_hbm
  146.0 1.0 copy.14.gt_hbm
  147.0 0.5 and_select_fusion.sources
  147.5 1.2 fusion.q_hbm
  148.8 47.4 %all-to-all-done.x_hbm = bf16[128,32,512]{2,1,0:T(8,128)(2,1)} async-done(((bf16[128,32,512]{2,1,0:T(8,128)(2,1)}), bf16[128,32,512]{2,1,0:T(8,128)(2,1)}, u32[]{:S(2)}, u32[]{:S(2)}) %all-to-all-start) | async-done | bytes 4194336 | tf_op jit(solution)/shard_map/all_to_all | solution.py:381
  196.2 19.2 %forward.1 = (bf16[4096,512]{1,0:T(8,128)(2,1)}, bf16[4096,512]{1,0:T(8,128)(2,1)}, f32[4,8,256]{2,1,0:T(8,128)}, bf16[128,16,128]{2,1,0:T(8,128)(2,1)}) custom-call(s32[128]{0:T(128)} %and_select_fusion.sources, s32[4]{0:T(128)} %dynamic_slice.7.counts, bf16[128,32,512]{2,1,0:T(8,128)(2,1)} %all-to-all-done.x_hbm, bf16[512,512]{1,0:T(8,128)(2,1)} %fusion.q_hbm, ...), custom_call_target="tpu_custom_call" | custom-call | flops 10000000000 | bytes 8388608 | tf_op jit(solution)/shard_map/forward/pallas_call | solution.py:253
  215.4 3.9 %all-to-all-start.1 = ((bf16[128,16,128]{2,1,0:T(8,128)(2,1)}), bf16[128,16,128]{2,1,0:T(8,128)(2,1)S(1)}, u32[]{:S(2)}, u32[]{:S(2)}) async-start(bf16[128,16,128]{2,1,0:T(8,128)(2,1)} %get-tuple-element.10), calls=%async_computation.1 | async-start | bytes 1048576 | tf_op jit(solution)/shard_map/all_to_all | solution.py:381
  219.3 24.1 %backward.1 = (bf16[128,144,128]{2,1,0:T(8,128)(2,1)}, bf16[512,512]{1,0:T(8,128)(2,1)}) custom-call(s32[128]{0:T(128)} %and_select_fusion.sources, s32[4]{0:T(128)} %dynamic_slice.7.counts, bf16[4096,512]{1,0:T(8,128)(2,1)} %get-tuple-element.11.k_hbm, bf16[4096,512]{1,0:T(8,128)(2,1)} %get-tuple-element.12.v_hbm, bf16[512,512]{1,0:T(8,128)(2,1)} %fusion.q_hbm, ...), custom_call_target="tpu_custom_call" | custom-call | flops 20000000000 | bytes 16777216 | tf_op jit(solution)/shard_map/backward/pallas_call | solution.py:292
  243.4 0.8 copy-done.3
  244.2 2.1 finish.1
  246.3 10.3 %all-to-all-start.2 = ((bf16[128,144,128]{2,1,0:T(8,128)(2,1)}), bf16[128,144,128]{2,1,0:T(8,128)(2,1)}, u32[]{:S(2)}, u32[]{:S(2)}) async-start(bf16[128,144,128]{2,1,0:T(8,128)(2,1)} %finish.1), calls=%async_computation.2 | async-start | bytes 9437184 | tf_op jit(solution)/shard_map/all_to_all | solution.py:381
  256.6 0.5 fusion.9
  257.1 58.2 %all-to-all-done.2.back_hbm = bf16[128,144,128]{2,1,0:T(8,128)(2,1)} async-done(((bf16[128,144,128]{2,1,0:T(8,128)(2,1)}), bf16[128,144,128]{2,1,0:T(8,128)(2,1)}, u32[]{:S(2)}, u32[]{:S(2)}) %all-to-all-start.2) | async-done | bytes 4718624 | tf_op jit(solution)/shard_map/all_to_all | solution.py:381
  315.3 4.6 %combine.1 = (bf16[16,32,512]{2,1,0:T(8,128)(2,1)}, f32[512,512]{1,0:T(8,128)}) custom-call(s32[128]{0:T(128)S(1)} %copy-done.1, bf16[128,144,128]{2,1,0:T(8,128)(2,1)} %all-to-all-done.2.back_hbm, f32[16,32,512]{2,1,0:T(8,128)S(1)} %bitcast.14), custom_call_target="tpu_custom_call" | custom-call | tf_op jit(solution)/shard_map/combine/pallas_call | solution.py:432
  (15 shorter events, 0.0 us)
Async XLA Ops:
  0.6 146.9 %copy-start = (bf16[512,512]{1,0:T(8,128)(2,1)S(1)}, bf16[512,512]{1,0:T(8,128)(2,1)}, u32[]{:S(2)}) copy-start(bf16[512,512]{1,0:T(8,128)(2,1)} %param.10) | copy-start | bytes 1572868
  131.2 14.3 %copy-start.4 = (bf16[512,512]{1,0:T(8,128)(2,1)S(1)}, bf16[512,512]{1,0:T(8,128)(2,1)}, u32[]{:S(2)}) copy-start(bf16[512,512]{1,0:T(8,128)(2,1)} %param.13) | copy-start | bytes 1572868
  131.2 14.3 %copy-start.6 = (bf16[1,512,512]{2,1,0:T(8,128)(2,1)S(1)}, bf16[1,512,512]{2,1,0:T(8,128)(2,1)}, u32[]{:S(2)}) copy-start(bf16[1,512,512]{2,1,0:T(8,128)(2,1)} %param.9) | copy-start | bytes 1572868
  131.2 16.3 %copy-start.5 = (bf16[1,512,512]{2,1,0:T(8,128)(2,1)S(1)}, bf16[1,512,512]{2,1,0:T(8,128)(2,1)}, u32[]{:S(2)}) copy-start(bf16[1,512,512]{2,1,0:T(8,128)(2,1)} %param.8) | copy-start | bytes 1572868
  131.3 64.9 %all-to-all-start = ((bf16[128,32,512]{2,1,0:T(8,128)(2,1)}), bf16[128,32,512]{2,1,0:T(8,128)(2,1)}, u32[]{:S(2)}, u32[]{:S(2)}) async-start(bf16[128,32,512]{2,1,0:T(8,128)(2,1)} %gather.1), calls=%async_computation | async-start | bytes 8388608 | tf_op jit(solution)/shard_map/all_to_all | solution.py:381
  146.0 69.4 %copy-start.2 = (bf16[512,512]{1,0:T(8,128)(2,1)}, bf16[512,512]{1,0:T(8,128)(2,1)S(1)}, u32[]{:S(2)}) copy-start(bf16[512,512]{1,0:T(8,128)(2,1)S(1)} %convolution_convert_fusion.g_hbm) | copy-start | bytes 1572868
  215.4 28.0 %all-to-all-start.1 = ((bf16[128,16,128]{2,1,0:T(8,128)(2,1)}), bf16[128,16,128]{2,1,0:T(8,128)(2,1)S(1)}, u32[]{:S(2)}, u32[]{:S(2)}) async-start(bf16[128,16,128]{2,1,0:T(8,128)(2,1)} %get-tuple-element.10), calls=%async_computation.1 | async-start | bytes 1048576 | tf_op jit(solution)/shard_map/all_to_all | solution.py:381
  243.4 0.8 copy-start.3
  246.3 10.3 %copy-start.7 = (bf16[512,512]{1,0:T(8,128)(2,1)S(1)}, bf16[512,512]{1,0:T(8,128)(2,1)}, u32[]{:S(2)}) copy-start(bf16[512,512]{1,0:T(8,128)(2,1)} %get-tuple-element.15) | copy-start | bytes 1572868
  246.3 69.0 %copy-start.1 = (s32[128]{0:T(128)S(1)}, s32[128]{0:T(128)}, u32[]{:S(2)}) copy-start(s32[128]{0:T(128)} %reduce_max.18.wanted) | copy-start | bytes 1540
  246.3 69.0 %all-to-all-start.2 = ((bf16[128,144,128]{2,1,0:T(8,128)(2,1)}), bf16[128,144,128]{2,1,0:T(8,128)(2,1)}, u32[]{:S(2)}, u32[]{:S(2)}) async-start(bf16[128,144,128]{2,1,0:T(8,128)(2,1)} %finish.1), calls=%async_computation.2 | async-start | bytes 9437184 | tf_op jit(solution)/shard_map/all_to_all | solution.py:381

commit v3 on v2

v3 whole, which is shorter than its diff:
```python
import jax
import jax.numpy as jnp
from jax import lax
from jax.experimental import pallas as pl
from jax.experimental.pallas import tpu as pltpu
from jax.sharding import PartitionSpec as P

HEAD_DIM = 64
QUERY_BLOCK = 128
KEY_SEG = 32
MAXK = 32
AXES = ("view", "row")
SPAN = MAXK * KEY_SEG
PAIR = 2 * HEAD_DIM
BOTH = 2 * QUERY_BLOCK
LANES = 128
MIB = 1024 * 1024
F32 = jnp.float32
BF16 = jnp.bfloat16
FWD_ROWS = 256
BWD_ROWS = 256
PROJ_ROWS = 256
PROJ_COLS = 256

def dot(a, b, ca=1, cb=0):
    return lax.dot_general(a, b, (((ca,), (cb,)), ((), ())), preferred_element_type=F32)

def split_heads(rows):
    low_half = lax.broadcasted_iota(jnp.int32, rows.shape, 1) < HEAD_DIM
    zero = jnp.zeros_like(rows)
    return jnp.concatenate(
        [jnp.where(low_half, rows, zero), jnp.where(low_half, zero, rows)], axis=0)

def split_channels(cols):
    zero = jnp.zeros((HEAD_DIM, QUERY_BLOCK), cols.dtype)
    return jnp.concatenate(
        [
            jnp.concatenate([cols[:HEAD_DIM], zero], axis=1),
            jnp.concatenate([zero, cols[HEAD_DIM:]], axis=1),
        ],
        axis=0,
    )


def fold(rows, op):
    return op(rows.reshape(rows.shape[0] // 8, 8, rows.shape[-1]), axis=0)

def masked_scores(k_rows, qb, live_rows, start):
    s = dot(k_rows, qb)
    ids = lax.broadcasted_iota(jnp.int32, s.shape, 0)
    return jnp.where(ids < live_rows - start, s, F32(-1e30))

def forward_kernel(
    sources, counts, x_hbm, qt_hbm, gt_hbm, wk_hbm, wv_hbm, dy_hbm,
    k_out, v_out, stat_ref, grad_ref,
    xg, ks, vs, ss, ps, att, qt_ref, gt_ref, wk_ref, wv_ref, dy_ref, sems, osems, wsems,
):
    blocks = qt_ref.shape[1] // QUERY_BLOCK
    width = x_hbm.shape[-1]
    pairs = width // PAIR

    def fetch(b):
        def one(j, carry):
            pltpu.make_async_copy(
                x_hbm.at[sources[b * MAXK + j]], xg.at[b * MAXK + j], sems.at[b]
            ).start()
            return carry
        lax.fori_loop(0, MAXK, one, 0, unroll=8)

    weights = [(wk_hbm, wk_ref), (wv_hbm, wv_ref), (qt_hbm, qt_ref), (gt_hbm, gt_ref), (dy_hbm, dy_ref)]
    loads = [pltpu.make_async_copy(a, z, wsems.at[i]) for i, (a, z) in enumerate(weights)]
    loads[0].start()
    loads[1].start()
    fetch(0)
    for load in loads[2:]:
        load.start()
    loads[0].wait()
    loads[1].wait()

    ncol = 2 * width // PROJ_COLS

    def project(b, c):
        if c == 0:
            mine = xg.at[pl.ds(b * MAXK, MAXK)]
            pltpu.make_async_copy(mine, mine, sems.at[b]).wait()
        half = ncol // 2
        w_ref, dst, hbm, sem = (
            (wk_ref, ks, k_out, osems.at[0]) if c < half else (wv_ref, vs, v_out, osems.at[1])
        )
        cols = pl.ds((c % half) * PROJ_COLS, PROJ_COLS)
        span = pl.ds(b * SPAN, SPAN)
        segs = PROJ_ROWS // KEY_SEG
        for r in range(SPAN // PROJ_ROWS):
            part = xg[pl.ds(b * MAXK + r * segs, segs)].reshape(PROJ_ROWS, width)
            dst[pl.ds(b * SPAN + r * PROJ_ROWS, PROJ_ROWS), cols] = dot(part, w_ref[:, cols]).astype(BF16)
        if c % half == half - 1:
            pltpu.make_async_copy(dst.at[span], hbm.at[span], sem).start()

    state = {}

    def scores(b, p):
        cols = pl.ds(p * PAIR, PAIR)
        tok = pl.ds(b * QUERY_BLOCK, QUERY_BLOCK)
        live_rows = counts[b] * KEY_SEG
        slot = (b * pairs + p) % 2
        qb = split_channels(qt_ref[cols, tok])
        state["top", b, p] = jnp.full((8, BOTH), -1e30, F32)

        def chunk(c):
            rows = pl.ds(c * FWD_ROWS, FWD_ROWS)
            s = masked_scores(ks[pl.ds(b * SPAN + c * FWD_ROWS, FWD_ROWS), cols], qb, live_rows, c * FWD_ROWS)
            ss[slot, rows, :] = s
            state["top", b, p] = jnp.maximum(state["top", b, p], fold(s, jnp.max))

        return [lambda c=c: chunk(c) for c in range(SPAN // FWD_ROWS)]

    def attend(b, p):
        slot = (b * pairs + p) % 2
        top = jnp.max(state["top", b, p], axis=0, keepdims=True)
        state["top", b, p] = top
        state["sum", b, p] = jnp.zeros((8, BOTH), F32)

        def chunk(c):
            rows = pl.ds(c * FWD_ROWS, FWD_ROWS)
            e = jnp.exp(ss[slot, rows, :] - top)
            ps[slot, rows, :] = e.astype(BF16)
            state["sum", b, p] = state["sum", b, p] + fold(e, jnp.sum)

        return [lambda c=c: chunk(c) for c in range(SPAN // FWD_ROWS)]

    def collect(b, p):
        cols = pl.ds(p * PAIR, PAIR)
        tok = pl.ds(b * QUERY_BLOCK, QUERY_BLOCK)
        slot = (b * pairs + p) % 2
        total = jnp.sum(state["sum", b, p], axis=0, keepdims=True)
        inverse = 1.0 / total
        out = dot(vs[pl.ds(b * SPAN, SPAN), cols], ps[slot], 0, 0)
        deltas = []
        for h in range(2):
            here = out[h * HEAD_DIM:(h + 1) * HEAD_DIM, h * QUERY_BLOCK:(h + 1) * QUERY_BLOCK]
            here = here * inverse[:, h * QUERY_BLOCK:(h + 1) * QUERY_BLOCK]
            here = here.astype(BF16)
            chan = pl.ds(p * PAIR + h * HEAD_DIM, HEAD_DIM)
            att[chan, tok] = here
            both = here.astype(F32) * gt_ref[chan, tok].astype(F32)
            deltas.append(jnp.sum(both, axis=0, keepdims=True))
        stat_ref[b, pl.ds(p, 1), :] = state["top", b, p] + jnp.log(total)
        stat_ref[b, pl.ds(pairs + p, 1), :] = jnp.concatenate(deltas, axis=1)

    for b in range(1, blocks):
        fetch(b)
    for c in range(ncol):
        project(0, c)
    for load in loads[2:]:
        load.wait()
    steps = [(b, p) for b in range(blocks) for p in range(pairs)]
    each = ncol // pairs
    for part in scores(*steps[0]):
        part()
    for i, (b, p) in enumerate(steps):
        more = []
        if i + 1 < len(steps):
            if p + 1 == pairs:
                for c in range((pairs - 1) * each, ncol):
                    project(b + 1, c)
            more = scores(*steps[i + 1])
        now = attend(b, p)
        for c in range(len(now)):
            if more and c < len(more):
                more[c]()
            now[c]()
        if b + 1 < blocks and p + 1 < pairs:
            for c in range(p * each, (p + 1) * each):
                project(b + 1, c)
        collect(b, p)
    per = grad_ref.shape[1]
    slots = width // LANES
    for r in range(width // 128):
        g = dot(att[pl.ds(r * 128, 128), :], dy_ref[...]).astype(BF16)
        for i in range(128 // per):
            for t in range(slots):
                grad_ref[(r * (128 // per) + i) * slots + t] = g[
                    i * per:(i + 1) * per, t * LANES:(t + 1) * LANES
                ]
    pltpu.make_async_copy(ks, k_out, osems.at[0]).wait()
    pltpu.make_async_copy(vs, v_out, osems.at[1]).wait()


def backward_kernel(
    sources, counts, first, last, k_hbm, v_hbm, q_hbm, g_hbm, qt_hbm, gt_hbm, stat_ref, wk_hbm, wv_hbm,
    ret_hbm, dq_ref,
    ks, vs, ps, ds, dk, dv, acc, q_ref, g_ref, qt_ref, gt_ref, wk_ref, wv_ref, out, sems, wsems, osem,
):
    blocks = q_ref.shape[0] // QUERY_BLOCK
    width = wk_ref.shape[-1]
    pairs = width // PAIR
    devices = acc.shape[0]
    weights = [
        (qt_hbm, qt_ref), (gt_hbm, gt_ref), (q_hbm, q_ref), (g_hbm, g_ref),
        (wk_hbm, wk_ref), (wv_hbm, wv_ref),
    ]
    loads = [pltpu.make_async_copy(a, z, wsems.at[i]) for i, (a, z) in enumerate(weights)]

    def fetch(b):
        span = pl.ds(b * SPAN, SPAN)
        pltpu.make_async_copy(k_hbm.at[span], ks.at[span], sems.at[b, 0]).start()
        pltpu.make_async_copy(v_hbm.at[span], vs.at[span], sems.at[b, 1]).start()

    loads[0].start()
    loads[1].start()
    fetch(0)
    for load in loads[2:]:
        load.start()
    for b in range(1, blocks):
        fetch(b)
    loads[0].wait()
    loads[1].wait()

    def soft(b, p):
        if p == 0:
            span = pl.ds(b * SPAN, SPAN)
            pltpu.make_async_copy(ks.at[span], ks.at[span], sems.at[b, 0]).wait()
            pltpu.make_async_copy(vs.at[span], vs.at[span], sems.at[b, 1]).wait()
        tok = pl.ds(b * QUERY_BLOCK, QUERY_BLOCK)
        live_rows = counts[b] * KEY_SEG
        slot = (b * pairs + p) % 2
        cols = pl.ds(p * PAIR, PAIR)
        qb = split_channels(qt_ref[cols, tok])
        gb = split_channels(gt_ref[cols, tok])
        lse = stat_ref[b, pl.ds(p, 1), :]
        delta = stat_ref[b, pl.ds(pairs + p, 1), :]

        def chunk(c):
            rows = pl.ds(c * BWD_ROWS, BWD_ROWS)
            there = pl.ds(b * SPAN + c * BWD_ROWS, BWD_ROWS)
            s = masked_scores(ks[there, cols], qb, live_rows, c * BWD_ROWS)
            dp = dot(vs[there, cols], gb)
            w = jnp.exp(s - lse)
            ps[slot, rows, :] = w.astype(BF16)
            ds[slot, rows, :] = (w * (dp - delta)).astype(BF16)

        return [lambda c=c: chunk(c) for c in range(SPAN // BWD_ROWS)]

    def grads(b, p):
        tok = pl.ds(b * QUERY_BLOCK, QUERY_BLOCK)
        slot = (b * pairs + p) % 2
        cols = pl.ds(p * PAIR, PAIR)
        qb = split_heads(q_ref[tok, cols])
        gb = split_heads(g_ref[tok, cols])

        def do_dv():
            dv[b % 2, :, cols] = dot(ps[slot], gb).astype(BF16)

        def do_dk():
            dk[b % 2, :, cols] = dot(ds[slot], qb).astype(BF16)

        def do_dq():
            dq = dot(ks[pl.ds(b * SPAN, SPAN), cols], ds[slot], 0, 0) * F32(HEAD_DIM ** -0.5)
            for h in range(2):
                here = dq[h * HEAD_DIM:(h + 1) * HEAD_DIM, h * QUERY_BLOCK:(h + 1) * QUERY_BLOCK]
                dq_ref[pl.ds(p * PAIR + h * HEAD_DIM, HEAD_DIM), tok] = here.astype(BF16)

        return [do_dv, do_dk, do_dq]

    lines = KEY_SEG * width // LANES
    per = SPAN // pairs
    segs = per // KEY_SEG

    def back(b, c):
        rows = pl.ds(c * per, per)
        term = dot(dk[b % 2, rows, :], wk_ref[...]) + dot(dv[b % 2, rows, :], wv_ref[...])
        for j in range(segs):
            entry = b * MAXK + c * segs + j
            slot = sources[entry]
            mine = term[j * KEY_SEG:(j + 1) * KEY_SEG, :]
            if b:
                mine = jnp.where(first[entry] > 0, mine, acc[slot] + mine)
            if b + 1 < blocks:
                acc[slot] = mine
            low = mine.astype(BF16)
            for u in range(width // LANES):
                out[slot, pl.ds(u * KEY_SEG, KEY_SEG), :] = low[:, u * LANES:(u + 1) * LANES]

    def line(entry):
        slot = sources[entry]
        return pltpu.make_async_copy(out.at[slot], ret_hbm.at[slot, pl.ds(0, lines)], osem)

    def send(start, size):
        def one(entry, carry):
            @pl.when(last[entry] > 0)
            def _():
                line(entry).start()

            return carry

        lax.fori_loop(start, start + size, one, 0, unroll=4)

    steps = [(b, p) for b in range(blocks) for p in range(pairs)]
    for i in range(len(steps) + 1):
        now = soft(*steps[i]) if i < len(steps) else []
        if i == 1:
            loads[2].wait()
            loads[3].wait()
        old = grads(*steps[i - 1]) if i else []
        for c in range(max(len(now), len(old))):
            if c < len(now):
                now[c]()
            if c < len(old):
                old[c]()
        if i == 1:
            for load in loads[4:]:
                load.wait()
        if i and steps[i - 1][0]:
            back(steps[i - 1][0] - 1, steps[i - 1][1])
            if steps[i - 1][1] == pairs - 1:
                send((steps[i - 1][0] - 1) * MAXK, MAXK)
    for p in range(pairs):
        back(blocks - 1, p)
        send((blocks - 1) * MAXK + p * segs, segs)

    def finish(entry, carry):
        @pl.when(last[entry] > 0)
        def _():
            line(entry).wait()

        return carry

    lax.fori_loop(0, blocks * MAXK, finish, 0, unroll=4)


VMEM = pl.BlockSpec(memory_space=pltpu.VMEM)
SMEM = pl.BlockSpec(memory_space=pltpu.SMEM)
ANY = pl.BlockSpec(memory_space=pl.ANY)

def square(width, tokens):
    return pltpu.VMEM((tokens, width), BF16)

def forward(sources, counts, fetched, queries_t, grad_out_t, w_key, w_value, grads):
    devices, _, width = fetched.shape
    tokens = queries_t.shape[1]
    blocks = tokens // QUERY_BLOCK
    keys = blocks * SPAN
    per = width * width // (devices * LANES)
    return pl.pallas_call(
        forward_kernel,
        out_shape=[
            jax.ShapeDtypeStruct((keys, width), BF16),
            jax.ShapeDtypeStruct((keys, width), BF16),
            jax.ShapeDtypeStruct((blocks, 2 * width // PAIR, BOTH), F32),
            jax.ShapeDtypeStruct((devices, per, LANES), BF16),
        ],
        in_specs=[SMEM, SMEM] + [ANY] * 6,
        out_specs=[ANY, ANY, VMEM, VMEM],
        scratch_shapes=[
            pltpu.VMEM((blocks * MAXK, KEY_SEG, width), BF16),
            pltpu.VMEM((keys, width), BF16),
            pltpu.VMEM((keys, width), BF16),
            pltpu.VMEM((2, SPAN, BOTH), F32),
            pltpu.VMEM((2, SPAN, BOTH), BF16),
            pltpu.VMEM((width, tokens), BF16),
            pltpu.VMEM((tokens, width), BF16),
            pltpu.VMEM((width, tokens), BF16),
            pltpu.VMEM((width, width), BF16),
            pltpu.VMEM((width, width), BF16),
            pltpu.VMEM((tokens, width), BF16),
            pltpu.SemaphoreType.DMA((blocks,)),
            pltpu.SemaphoreType.DMA((2,)),
            pltpu.SemaphoreType.DMA((5,)),
        ],
        compiler_params=pltpu.CompilerParams(vmem_limit_bytes=60 * MIB),
        cost_estimate=pl.CostEstimate(
            flops=10_000_000_000, bytes_accessed=8 * MIB, transcendentals=4 * MIB),
        name="forward",
    )(sources, counts, fetched, queries_t, grad_out_t, w_key, w_value, grads)


def backward(sources, counts, first, last, keys, values, queries, grad_out, queries_t, grad_out_t, stats, w_key, w_value, devices):
    tokens, width = queries.shape
    blocks = tokens // QUERY_BLOCK
    lines = KEY_SEG * width // LANES
    extra = width * width // (devices * LANES)
    return pl.pallas_call(
        backward_kernel,
        out_shape=[
            jax.ShapeDtypeStruct((devices, lines + extra, LANES), BF16),
            jax.ShapeDtypeStruct((width, tokens), BF16),
        ],
        in_specs=[SMEM] * 4 + [ANY] * 6 + [VMEM] + [ANY] * 2,
        out_specs=[ANY, VMEM],
        scratch_shapes=[
            pltpu.VMEM((blocks * SPAN, width), BF16),
            pltpu.VMEM((blocks * SPAN, width), BF16),
            pltpu.VMEM((2, SPAN, BOTH), BF16),
            pltpu.VMEM((2, SPAN, BOTH), BF16),
            pltpu.VMEM((2, SPAN, width), BF16),
            pltpu.VMEM((2, SPAN, width), BF16),
            pltpu.VMEM((devices, KEY_SEG, width), F32),
            pltpu.VMEM((tokens, width), BF16),
            pltpu.VMEM((tokens, width), BF16),
            pltpu.VMEM((width, tokens), BF16),
            pltpu.VMEM((width, tokens), BF16),
            pltpu.VMEM((width, width), BF16),
            pltpu.VMEM((width, width), BF16),
            pltpu.VMEM((devices, lines, LANES), BF16),
            pltpu.SemaphoreType.DMA((blocks, 2)),
            pltpu.SemaphoreType.DMA((6,)),
            pltpu.SemaphoreType.DMA,
        ],
        compiler_params=pltpu.CompilerParams(vmem_limit_bytes=60 * MIB),
        cost_estimate=pl.CostEstimate(
            flops=20_000_000_000, bytes_accessed=16 * MIB, transcendentals=4 * MIB),
        name="backward",
              )(sources, counts, first, last, keys, values, queries, grad_out, queries_t, grad_out_t, stats, w_key, w_value)


def gather_kernel(wanted, x_hbm, out_ref, x_ref, sems):
    load = pltpu.make_async_copy(x_hbm, x_ref, sems.at[0])
    load.start()
    load.wait()

    def step(i, carry):
        pltpu.make_async_copy(
            x_ref.at[jnp.maximum(wanted[i], 0)], out_ref.at[i], sems.at[1]
        ).start()
        return carry

    lax.fori_loop(0, out_ref.shape[0], step, 0, unroll=8)
    pltpu.make_async_copy(out_ref, out_ref, sems.at[1]).wait()


def finish_kernel(parts_ref, ret_in, ret_out, wide, sem):
    total = jnp.sum(parts_ref[...].astype(F32), axis=0)
    wide[...] = jnp.broadcast_to(total.astype(BF16)[None], wide.shape)
    extra = wide.shape[1]
    rows = pl.ds(ret_out.shape[1] - extra, extra)
    copy = pltpu.make_async_copy(wide, ret_out.at[:, rows], sem)
    copy.start()
    copy.wait()


def combine_kernel(wanted, back_hbm, base_ref, out_ref, grad_ref, back, acc, sems):
    devices, lines, _ = back.shape
    groups = sems.shape[0]
    size = devices // groups
    width = base_ref.shape[-1]
    slots = width // LANES
    extra = lines - KEY_SEG * slots

    def copy(t):
        part = pl.ds(t * size, size)
        return pltpu.make_async_copy(back_hbm.at[part], back.at[part], sems.at[t])

    for t in range(groups):
        copy(t).start()
    acc[...] = base_ref[...]
    for t in range(groups):
        copy(t).wait()

        def step(i, carry):
            seg = wanted[i]

            @pl.when(seg >= 0)
            def _():
                for u in range(slots):
                    cols = pl.ds(u * LANES, LANES)
                    acc[seg, :, cols] += back[i, pl.ds(u * KEY_SEG, KEY_SEG), :].astype(F32)

            return carry

        lax.fori_loop(t * size, (t + 1) * size, step, 0)
        for i in range(t * size, (t + 1) * size):
            rows = pl.ds((i // slots) * extra, extra)
            cols = pl.ds((i % slots) * LANES, LANES)
            grad_ref[rows, cols] = back[i, pl.ds(lines - extra, extra), :].astype(F32)
    out_ref[...] = acc[...].astype(out_ref.dtype)


def exchange(v):
    return lax.all_to_all(v, AXES, split_axis=0, concat_axis=0, tiled=True)


def local(views_x, dy, w_query, w_key, w_value, w_out, key_lists, key_counts):
    width = views_x.shape[-1]
    x = views_x.reshape(-1, width)
    grads = dy.reshape(-1, width)
    tokens = x.shape[0]
    devices = lax.axis_size(AXES)
    me = lax.axis_index(AXES)
    seg_dev = tokens // KEY_SEG
    blocks = tokens // QUERY_BLOCK
    columns = jnp.arange(MAXK, dtype=jnp.int32)
    live = columns[None, :] < key_counts[:, None]
    asked = live & (key_lists // seg_dev == me)
    wanted = jnp.max(
        jnp.where(asked, key_lists % seg_dev, -1).reshape(devices, blocks * MAXK), axis=1
    )
    outgoing = pl.pallas_call(
        gather_kernel,
        out_shape=jax.ShapeDtypeStruct((devices, KEY_SEG, width), BF16),
        in_specs=[SMEM, ANY],
        out_specs=ANY,
        scratch_shapes=[
            pltpu.VMEM((seg_dev, KEY_SEG, width), BF16),
            pltpu.SemaphoreType.DMA((2,)),
        ],
        name="gather",
    )(wanted, x.reshape(seg_dev, KEY_SEG, width))
    fetched = exchange(outgoing)

    queries = dot(x, w_query).astype(BF16) * BF16(HEAD_DIM ** -0.5)
    grad_out = dot(grads, w_out, 1, 1).astype(BF16)
    queries_t = queries.T
    grad_out_t = grad_out.T
    mine = lax.dynamic_slice_in_dim(key_lists, me * blocks, blocks, 0)
    counts = lax.dynamic_slice_in_dim(key_counts, me * blocks, blocks, 0)
    sources = jnp.where(columns[None, :] < counts[:, None], mine // seg_dev, me).reshape(-1)
    entry = jnp.arange(blocks * MAXK, dtype=jnp.int32)
    same = sources[:, None] == sources[None, :]
    first = 1 - jnp.any(same & (entry[None, :] < entry[:, None]), axis=1).astype(jnp.int32)
    last = 1 - jnp.any(same & (entry[None, :] > entry[:, None]), axis=1).astype(jnp.int32)
    keys, values, stats, pieces = forward(
        sources, counts, fetched, queries_t, grad_out_t, w_key, w_value, grads
    )
    parts = exchange(pieces)
    ret, dq_t = backward(
        sources, counts, first, last, keys, values, queries, grad_out, queries_t, grad_out_t,
        stats, w_key.T, w_value.T, devices
    )
    ret = pl.pallas_call(
        finish_kernel,
        out_shape=jax.ShapeDtypeStruct(ret.shape, ret.dtype),
        in_specs=[VMEM, ANY],
        out_specs=ANY,
        scratch_shapes=[pltpu.VMEM(parts.shape, BF16), pltpu.SemaphoreType.DMA],
        input_output_aliases={1: 0},
        name="finish",
    )(parts, ret)
    back = exchange(ret)
    base = dot(dq_t, w_query, 0, 1)
    grad_x, grad_w_out = pl.pallas_call(
        combine_kernel,
        out_shape=[
            jax.ShapeDtypeStruct((seg_dev, KEY_SEG, width), BF16),
            jax.ShapeDtypeStruct((width, width), F32),
        ],
        in_specs=[SMEM, ANY, VMEM],
        out_specs=[VMEM, VMEM],
        scratch_shapes=[
            pltpu.VMEM(ret.shape, BF16),
            pltpu.VMEM((seg_dev, KEY_SEG, width), F32),
            pltpu.SemaphoreType.DMA((8,)),
        ],
        compiler_params=pltpu.CompilerParams(vmem_limit_bytes=24 * MIB),
        name="combine",
    )(wanted, back, base.reshape(seg_dev, KEY_SEG, width))
    return grad_x.reshape(views_x.shape), grad_w_out


def solution(mesh):
    in_specs = (P("view", "row", None), P("view", "row", None), P(), P(), P(), P(), P(), P())
    out_specs = (P("view", "row", None), P())
    return jax.shard_map(local, mesh=mesh, in_specs=in_specs, out_specs=out_specs, check_vma=False)
```

time: 321 us -> 191 us (0.60)
  Pallas kernels: 179 us -> 47 us
  waiting for transfers between devices: 106 us -> 102 us
    pallas_call x1, Pallas kernels: 129 us -> 3.68 us  [local(): pl.pallas_call(gather_kernel, out_shape=jax.ShapeDtypeStruct((devices, KE...]
    pallas_call x1, Pallas kernels: 19.2 us -> 14.3 us  [forward(): pl.pallas_call(forward_kernel, out_shape=[jax.ShapeDtypeStruct((keys, wid...]
    all_to_all x3, waiting for transfers between devices: 106 us -> 102 us  [exchange(): return lax.all_to_all(v, AXES, split_axis=0, concat_axis=0, tiled=True)]
  transfers between devices with their start and end apart: 3 -> 3, of which waited for: 2 -> 2; matrix products, arithmetic and copies ran while one was open for 2% -> 5% of each run, Pallas kernels for 8% -> 12%
where the time goes in v3:
time: 191 us; the launch traced here: 190 us
  waiting for transfers between devices  102 us (53%)
  Pallas kernels  47 us (25%)
  starting transfers between devices  28.2 us (15%)
  local copies, waits for them, and re-layouts  7.05 us (4%)
  other arithmetic  3.23 us (2%)
  matrix products  2.24 us (1%)
    all_to_all x3, waiting for transfers between devices, exchange(): return lax.all_to_all(v, AXES, split_axis=0, concat_axis=0, tiled=True)  102 us
    all_to_all x3, starting transfers between devices, exchange(): return lax.all_to_all(v, AXES, split_axis=0, concat_axis=0, tiled=True)  28.2 us
    pallas_call x1, Pallas kernels, backward(): pl.pallas_call(backward_kernel, out_shape=[jax.ShapeDtypeStruct((devices,...  22.3 us
    pallas_call x1, Pallas kernels, forward(): pl.pallas_call(forward_kernel, out_shape=[jax.ShapeDtypeStruct((keys, wid...  14.3 us
    pallas_call x1, Pallas kernels, local(): pl.pallas_call(combine_kernel, out_shape=[jax.ShapeDtypeStruct((seg_dev,...  4.69 us
  transfers between devices with their start and end apart: 3, of which 2 were waited for; matrix products, arithmetic and copies ran while one was open for 5% of the time, Pallas kernels for 12%

profile of v3, /device:TPU:1, one launch (start us, length us, event | category | flops | bytes accessed | tf_op | source)
XLA Modules:
  0.0 190.4 jit_solution(98561756282244849)
XLA Ops:
  0.7 1.0 fusion.4
  1.7 0.7 reduce_max.18.wanted
  2.4 3.7 %gather.1 = bf16[128,32,512]{2,1,0:T(8,128)(2,1)} custom-call(s32[128]{0:T(128)} %reduce_max.18.wanted, bf16[16,32,512]{2,1,0:T(8,128)(2,1)} %bitcast.20), custom_call_target="tpu_custom_call" | custom-call | tf_op jit(solution)/shard_map/gather/pallas_call | solution.py:497
  6.2 12.0 %all-to-all-start = ((bf16[128,32,512]{2,1,0:T(8,128)(2,1)}), bf16[128,32,512]{2,1,0:T(8,128)(2,1)}, u32[]{:S(2)}, u32[]{:S(2)}) async-start(bf16[128,32,512]{2,1,0:T(8,128)(2,1)} %gather.1), calls=%async_computation | async-start | bytes 8388608 | tf_op jit(solution)/shard_map/all_to_all | solution.py:479
  18.2 0.8 dynamic_slice.6.counts
  19.0 0.8 fusion.11
  20.0 1.3 fusion
  21.3 2.1 %copy.30.q_hbm = bf16[512,512]{1,0:T(8,128)(2,1)} copy(bf16[512,512]{0,1:T(8,128)(2,1)} %fusion) | data formatting | bytes 1048576 | tf_op jit(solution)/shard_map/mul | solution.py:510
  23.3 0.5 convolution_convert_fusion
  23.8 1.0 copy.31.g_hbm
  24.9 1.0 copy.28
  25.9 1.0 copy.29
  26.9 0.2 fusion.8
  27.0 0.6 convert_subtract_fusion
  27.6 43.5 %all-to-all-done.x_hbm = bf16[128,32,512]{2,1,0:T(8,128)(2,1)} async-done(((bf16[128,32,512]{2,1,0:T(8,128)(2,1)}), bf16[128,32,512]{2,1,0:T(8,128)(2,1)}, u32[]{:S(2)}, u32[]{:S(2)}) %all-to-all-start) | async-done | bytes 4194336 | tf_op jit(solution)/shard_map/all_to_all | solution.py:479
  71.1 14.3 %forward.1 = (bf16[4096,512]{1,0:T(8,128)(2,1)}, bf16[4096,512]{1,0:T(8,128)(2,1)}, f32[4,8,256]{2,1,0:T(8,128)}, bf16[128,16,128]{2,1,0:T(8,128)(2,1)}) custom-call(s32[128]{0:T(128)} %copy-done.10, s32[4]{0:T(128)} %copy-done.11, bf16[128,32,512]{2,1,0:T(8,128)(2,1)} %all-to-all-done.x_hbm, bf16[512,512]{1,0:T(8,128)(2,1)} %bitcast.22, ...), custom_call_target="tpu_custom_call" | custom-call | flops 10000000000 | bytes 8388608 | tf_op jit(solution)/shard_map/forward/pallas_call | solution.py:344
  85.4 6.0 %all-to-all-start.1 = ((bf16[128,16,128]{2,1,0:T(8,128)(2,1)}), bf16[128,16,128]{2,1,0:T(8,128)(2,1)S(1)}, u32[]{:S(2)}, u32[]{:S(2)}) async-start(bf16[128,16,128]{2,1,0:T(8,128)(2,1)} %get-tuple-element.10), calls=%async_computation.1 | async-start | bytes 1048576 | tf_op jit(solution)/shard_map/all_to_all | solution.py:479
  91.4 22.3 %backward.1 = (bf16[128,144,128]{2,1,0:T(8,128)(2,1)}, bf16[512,512]{1,0:T(8,128)(2,1)}) custom-call(s32[128]{0:T(128)} %copy-done.10, s32[4]{0:T(128)} %copy-done.11, s32[128]{0:T(128)} %get-tuple-element.21.first, s32[128]{0:T(128)} %get-tuple-element.20.last, bf16[4096,512]{1,0:T(8,128)(2,1)} %get-tuple-element.11.k_hbm, ...), custom_call_target="tpu_custom_call" | custom-call | flops 20000000000 | bytes 16777216 | tf_op jit(solution)/shard_map/backward/pallas_call | solution.py:382
  113.7 0.8 copy-done.3
  114.5 2.1 %finish.1 = bf16[128,144,128]{2,1,0:T(8,128)(2,1)} custom-call(bf16[128,16,128]{2,1,0:T(8,128)(2,1)} %copy-done.3, bf16[128,144,128]{2,1,0:T(8,128)(2,1)} %get-tuple-element.14.ret_in), custom_call_target="tpu_custom_call", output_to_operand_aliasing={{}: (1, {})} | custom-call | tf_op jit(solution)/shard_map/finish/pallas_call | solution.py:529
  116.6 10.2 %all-to-all-start.2 = ((bf16[128,144,128]{2,1,0:T(8,128)(2,1)}), bf16[128,144,128]{2,1,0:T(8,128)(2,1)}, u32[]{:S(2)}, u32[]{:S(2)}) async-start(bf16[128,144,128]{2,1,0:T(8,128)(2,1)} %finish.1), calls=%async_computation.2 | async-start | bytes 9437184 | tf_op jit(solution)/shard_map/all_to_all | solution.py:479
  126.8 0.5 fusion.14
  127.3 58.2 %all-to-all-done.2.back_hbm = bf16[128,144,128]{2,1,0:T(8,128)(2,1)} async-done(((bf16[128,144,128]{2,1,0:T(8,128)(2,1)}), bf16[128,144,128]{2,1,0:T(8,128)(2,1)}, u32[]{:S(2)}, u32[]{:S(2)}) %all-to-all-start.2) | async-done | bytes 4718624 | tf_op jit(solution)/shard_map/all_to_all | solution.py:479
  185.5 4.7 %combine.1 = (bf16[16,32,512]{2,1,0:T(8,128)(2,1)}, f32[512,512]{1,0:T(8,128)}) custom-call(s32[128]{0:T(128)S(1)} %copy-done.1, bf16[128,144,128]{2,1,0:T(8,128)(2,1)} %all-to-all-done.2.back_hbm, f32[16,32,512]{2,1,0:T(8,128)S(1)} %bitcast.17), custom_call_target="tpu_custom_call" | custom-call | tf_op jit(solution)/shard_map/combine/pallas_call | solution.py:540
  (27 shorter events, 0.3 us)
Async XLA Ops:
  0.6 19.4 %copy-start = (bf16[512,512]{1,0:T(8,128)(2,1)S(1)}, bf16[512,512]{1,0:T(8,128)(2,1)}, u32[]{:S(2)}) copy-start(bf16[512,512]{1,0:T(8,128)(2,1)} %param.10) | copy-start | bytes 1572868
  6.1 13.9 %copy-start.4 = (bf16[1,512,512]{2,1,0:T(8,128)(2,1)S(1)}, bf16[1,512,512]{2,1,0:T(8,128)(2,1)}, u32[]{:S(2)}) copy-start(bf16[1,512,512]{2,1,0:T(8,128)(2,1)} %param.8) | copy-start | bytes 1572868
  6.1 17.2 %copy-start.5 = (bf16[512,512]{1,0:T(8,128)(2,1)S(1)}, bf16[512,512]{1,0:T(8,128)(2,1)}, u32[]{:S(2)}) copy-start(bf16[512,512]{1,0:T(8,128)(2,1)} %param.13) | copy-start | bytes 1572868
  6.2 17.2 %copy-start.6 = (bf16[1,512,512]{2,1,0:T(8,128)(2,1)S(1)}, bf16[1,512,512]{2,1,0:T(8,128)(2,1)}, u32[]{:S(2)}) copy-start(bf16[1,512,512]{2,1,0:T(8,128)(2,1)} %param.9) | copy-start | bytes 1572868
  6.2 64.9 %all-to-all-start = ((bf16[128,32,512]{2,1,0:T(8,128)(2,1)}), bf16[128,32,512]{2,1,0:T(8,128)(2,1)}, u32[]{:S(2)}, u32[]{:S(2)}) async-start(bf16[128,32,512]{2,1,0:T(8,128)(2,1)} %gather.1), calls=%async_computation | async-start | bytes 8388608 | tf_op jit(solution)/shard_map/all_to_all | solution.py:479
  18.1 6.7 %copy-start.7 = (bf16[512,512]{1,0:T(8,128)(2,1)S(1)}, bf16[512,512]{1,0:T(8,128)(2,1)}, u32[]{:S(2)}) copy-start(bf16[512,512]{1,0:T(8,128)(2,1)} %wk_hbm.1) | copy-start | bytes 1572868
  18.1 7.7 %copy-start.8 = (bf16[512,512]{1,0:T(8,128)(2,1)S(1)}, bf16[512,512]{1,0:T(8,128)(2,1)}, u32[]{:S(2)}) copy-start(bf16[512,512]{1,0:T(8,128)(2,1)} %wv_hbm.1) | copy-start | bytes 1572868
  19.0 52.1 %copy-start.11 = (s32[4]{0:T(128)}, s32[4]{0:T(128)S(1)}, u32[]{:S(2)}) copy-start(s32[4]{0:T(128)S(1)} %dynamic_slice.6.counts) | copy-start | bytes 52
  20.0 51.1 %copy-start.10 = (s32[128]{0:T(128)}, s32[128]{0:T(128)S(1)}, u32[]{:S(2)}) copy-start(s32[128]{0:T(128)S(1)} %reshape.25.sources) | copy-start | bytes 1540
  23.8 47.3 %copy-start.2 = (bf16[512,512]{0,1:T(8,128)(2,1)}, bf16[512,512]{0,1:T(8,128)(2,1)S(1)}, u32[]{:S(2)}) copy-start(bf16[512,512]{0,1:T(8,128)(2,1)S(1)} %convolution_convert_fusion) | copy-start | bytes 1572868
  85.4 28.3 %all-to-all-start.1 = ((bf16[128,16,128]{2,1,0:T(8,128)(2,1)}), bf16[128,16,128]{2,1,0:T(8,128)(2,1)S(1)}, u32[]{:S(2)}, u32[]{:S(2)}) async-start(bf16[128,16,128]{2,1,0:T(8,128)(2,1)} %get-tuple-element.10), calls=%async_computation.1 | async-start | bytes 1048576 | tf_op jit(solution)/shard_map/all_to_all | solution.py:479
  113.7 0.8 copy-start.3
  116.6 10.2 %copy-start.9 = (bf16[512,512]{1,0:T(8,128)(2,1)S(1)}, bf16[512,512]{1,0:T(8,128)(2,1)}, u32[]{:S(2)}) copy-start(bf16[512,512]{1,0:T(8,128)(2,1)} %get-tuple-element.15) | copy-start | bytes 1572868
  116.6 68.9 %copy-start.1 = (s32[128]{0:T(128)S(1)}, s32[128]{0:T(128)}, u32[]{:S(2)}) copy-start(s32[128]{0:T(128)} %reduce_max.18.wanted) | copy-start | bytes 1540
  116.6 68.9 %all-to-all-start.2 = ((bf16[128,144,128]{2,1,0:T(8,128)(2,1)}), bf16[128,144,128]{2,1,0:T(8,128)(2,1)}, u32[]{:S(2)}, u32[]{:S(2)}) async-start(bf16[128,144,128]{2,1,0:T(8,128)(2,1)} %finish.1), calls=%async_computation.2 | async-start | bytes 9437184 | tf_op jit(solution)/shard_map/all_to_all | solution.py:479

commit v4 on v3

--- a/solution.py
+++ b/solution.py
@@ -413,22 +413,27 @@
               )(sources, counts, first, last, keys, values, queries, grad_out, queries_t, grad_out_t, stats, w_key, w_value)
 
 
-def gather_kernel(wanted, x_hbm, out_ref, x_ref, sems):
+def gather_kernel(block_max, x_hbm, out_ref, x_ref, sems):
     load = pltpu.make_async_copy(x_hbm, x_ref, sems.at[0])
     load.start()
     load.wait()
+    blocks = block_max.shape[0] // out_ref.shape[0]
 
     def step(i, carry):
-        pltpu.make_async_copy(
-            x_ref.at[jnp.maximum(wanted[i], 0)], out_ref.at[i], sems.at[1]
-        ).start()
+        seg = jnp.int32(0)
+        for k in range(blocks):
+            seg = jnp.maximum(seg, block_max[i * blocks + k])
+        pltpu.make_async_copy(x_ref.at[seg], out_ref.at[i], sems.at[1]).start()
         return carry
 
     lax.fori_loop(0, out_ref.shape[0], step, 0, unroll=8)
     pltpu.make_async_copy(out_ref, out_ref, sems.at[1]).wait()
 
 
-def finish_kernel(parts_ref, ret_in, ret_out, wide, sem):
+def finish_kernel(parts_hbm, ret_in, ret_out, parts_ref, wide, sem):
+    load = pltpu.make_async_copy(parts_hbm, parts_ref, sem)
+    load.start()
+    load.wait()
     total = jnp.sum(parts_ref[...].astype(F32), axis=0)
     wide[...] = jnp.broadcast_to(total.astype(BF16)[None], wide.shape)
     extra = wide.shape[1]
@@ -438,41 +443,54 @@
     copy.wait()
 
 
-def combine_kernel(wanted, back_hbm, base_ref, out_ref, grad_ref, back, acc, sems):
-    devices, lines, _ = back.shape
-    groups = sems.shape[0]
-    size = devices // groups
+def combine_kernel(
+    wanted, back_hbm, base_ref, out_hbm, grad_hbm, back, acc, wide, grad, out, sems, ends
+):
+    devices, extra, _ = wide.shape
     width = base_ref.shape[-1]
     slots = width // LANES
-    extra = lines - KEY_SEG * slots
-
-    def copy(t):
-        part = pl.ds(t * size, size)
-        return pltpu.make_async_copy(back_hbm.at[part], back.at[part], sems.at[t])
-
-    for t in range(groups):
-        copy(t).start()
+    lines = KEY_SEG * slots
+    tail = pltpu.make_async_copy(back_hbm.at[:, pl.ds(lines, extra)], wide, ends.at[0])
+    tail.start()
+
+    def line(i):
+        return pltpu.make_async_copy(back_hbm.at[i, pl.ds(0, lines)], back.at[i], sems.at[i])
+
+    def fetch(i, carry):
+        @pl.when(wanted[i] >= 0)
+        def _():
+            line(i).start()
+
+        return carry
+
+    lax.fori_loop(0, devices, fetch, 0, unroll=4)
     acc[...] = base_ref[...]
-    for t in range(groups):
-        copy(t).wait()
-
-        def step(i, carry):
-            seg = wanted[i]
-
-            @pl.when(seg >= 0)
-            def _():
-                for u in range(slots):
-                    cols = pl.ds(u * LANES, LANES)
-                    acc[seg, :, cols] += back[i, pl.ds(u * KEY_SEG, KEY_SEG), :].astype(F32)
-
-            return carry
-
-        lax.fori_loop(t * size, (t + 1) * size, step, 0)
-        for i in range(t * size, (t + 1) * size):
-            rows = pl.ds((i // slots) * extra, extra)
-            cols = pl.ds((i % slots) * LANES, LANES)
-            grad_ref[rows, cols] = back[i, pl.ds(lines - extra, extra), :].astype(F32)
-    out_ref[...] = acc[...].astype(out_ref.dtype)
+    tail.wait()
+    for i in range(devices):
+        rows = pl.ds((i // slots) * extra, extra)
+        cols = pl.ds((i % slots) * LANES, LANES)
+        grad[rows, cols] = wide[i].astype(F32)
+    grad_out = pltpu.make_async_copy(grad, grad_hbm, ends.at[1])
+    grad_out.start()
+
+    def add(i, carry):
+        seg = wanted[i]
+
+        @pl.when(seg >= 0)
+        def _():
+            line(i).wait()
+            for u in range(slots):
+                cols = pl.ds(u * LANES, LANES)
+                acc[seg, :, cols] += back[i, pl.ds(u * KEY_SEG, KEY_SEG), :].astype(F32)
+
+        return carry
+
+    lax.fori_loop(0, devices, add, 0)
+    out[...] = acc[...].astype(out.dtype)
+    x_out = pltpu.make_async_copy(out, out_hbm, ends.at[2])
+    x_out.start()
+    x_out.wait()
+    grad_out.wait()
 
 
 def exchange(v):
@@ -491,9 +509,8 @@
     columns = jnp.arange(MAXK, dtype=jnp.int32)
     live = columns[None, :] < key_counts[:, None]
     asked = live & (key_lists // seg_dev == me)
-    wanted = jnp.max(
-        jnp.where(asked, key_lists % seg_dev, -1).reshape(devices, blocks * MAXK), axis=1
-    )
+    block_max = jnp.max(jnp.where(asked, key_lists % seg_dev, -1), axis=1)
+    wanted = jnp.max(block_max.reshape(devices, blocks), axis=1)
     outgoing = pl.pallas_call(
         gather_kernel,
         out_shape=jax.ShapeDtypeStruct((devices, KEY_SEG, width), BF16),
@@ -504,7 +521,7 @@
             pltpu.SemaphoreType.DMA((2,)),
         ],
         name="gather",
-    )(wanted, x.reshape(seg_dev, KEY_SEG, width))
+    )(block_max, x.reshape(seg_dev, KEY_SEG, width))
     fetched = exchange(outgoing)
 
     queries = dot(x, w_query).astype(BF16) * BF16(HEAD_DIM ** -0.5)
@@ -529,10 +546,15 @@
     ret = pl.pallas_call(
         finish_kernel,
         out_shape=jax.ShapeDtypeStruct(ret.shape, ret.dtype),
-        in_specs=[VMEM, ANY],
+        in_specs=[ANY, ANY],
         out_specs=ANY,
-        scratch_shapes=[pltpu.VMEM(parts.shape, BF16), pltpu.SemaphoreType.DMA],
+        scratch_shapes=[
+            pltpu.VMEM(parts.shape, BF16),
+            pltpu.VMEM(parts.shape, BF16),
+            pltpu.SemaphoreType.DMA,
+        ],
         input_output_aliases={1: 0},
+        compiler_params=pltpu.CompilerParams(vmem_limit_bytes=60 * MIB),
         name="finish",
     )(parts, ret)
     back = exchange(ret)
@@ -544,11 +566,15 @@
             jax.ShapeDtypeStruct((width, width), F32),
         ],
         in_specs=[SMEM, ANY, VMEM],
-        out_specs=[VMEM, VMEM],
+        out_specs=[ANY, ANY],
         scratch_shapes=[
-            pltpu.VMEM(ret.shape, BF16),
+            pltpu.VMEM((devices, KEY_SEG * width // LANES, LANES), BF16),
             pltpu.VMEM((seg_dev, KEY_SEG, width), F32),
-            pltpu.SemaphoreType.DMA((8,)),
+            pltpu.VMEM(parts.shape, BF16),
+            pltpu.VMEM((width, width), F32),
+            pltpu.VMEM((seg_dev, KEY_SEG, width), BF16),
+            pltpu.SemaphoreType.DMA((devices,)),
+            pltpu.SemaphoreType.DMA((3,)),
         ],
         compiler_params=pltpu.CompilerParams(vmem_limit_bytes=24 * MIB),
         name="combine",

time: 191 us -> 192 us (level)
  Pallas kernels: 47 us -> 50.3 us
  starting transfers between devices: 28.2 us -> 25.8 us
    all_to_all x3, starting transfers between devices: 28.2 us -> 25.8 us  [exchange(): return lax.all_to_all(v, AXES, split_axis=0, concat_axis=0, tiled=True)]
    pallas_call x1, Pallas kernels: 14.3 us -> 16.6 us  [forward(): pl.pallas_call(forward_kernel, out_shape=[jax.ShapeDtypeStruct((keys, wid...]
where the time goes in v4:
time: 192 us; the launch traced here: 191 us
  waiting for transfers between devices  101 us (53%)
  Pallas kernels  50.3 us (26%)
  starting transfers between devices  25.8 us (13%)
  local copies, waits for them, and re-layouts  7.04 us (4%)
  other arithmetic  3.23 us (2%)
  matrix products  2.23 us (1%)
    all_to_all x3, waiting for transfers between devices, exchange(): return lax.all_to_all(v, AXES, split_axis=0, concat_axis=0, tiled=True)  101 us
    all_to_all x3, starting transfers between devices, exchange(): return lax.all_to_all(v, AXES, split_axis=0, concat_axis=0, tiled=True)  25.8 us
    pallas_call x1, Pallas kernels, backward(): pl.pallas_call(backward_kernel, out_shape=[jax.ShapeDtypeStruct((devices,...  22.3 us
    pallas_call x1, Pallas kernels, forward(): pl.pallas_call(forward_kernel, out_shape=[jax.ShapeDtypeStruct((keys, wid...  16.6 us
    pallas_call x1, Pallas kernels, local(): pl.pallas_call(combine_kernel, out_shape=[jax.ShapeDtypeStruct((seg_dev,...  5.66 us
  transfers between devices with their start and end apart: 3, of which 2 were waited for; matrix products, arithmetic and copies ran while one was open for 5% of the time, Pallas kernels for 12%

profile of v4, /device:TPU:1, one launch (start us, length us, event | category | flops | bytes accessed | tf_op | source)
XLA Modules:
  0.0 191.1 jit_solution(981004476396890109)
XLA Ops:
  0.7 1.6 fusion.4.block_max
  2.2 3.7 %gather.1 = bf16[128,32,512]{2,1,0:T(8,128)(2,1)} custom-call(s32[512]{0:T(512)} %fusion.4.block_max, bf16[16,32,512]{2,1,0:T(8,128)(2,1)} %bitcast.20), custom_call_target="tpu_custom_call" | custom-call | tf_op jit(solution)/shard_map/gather/pallas_call | solution.py:514
  6.0 12.0 %all-to-all-start = ((bf16[128,32,512]{2,1,0:T(8,128)(2,1)}), bf16[128,32,512]{2,1,0:T(8,128)(2,1)}, u32[]{:S(2)}, u32[]{:S(2)}) async-start(bf16[128,32,512]{2,1,0:T(8,128)(2,1)} %gather.1), calls=%async_computation | async-start | bytes 8388608 | tf_op jit(solution)/shard_map/all_to_all | solution.py:497
  18.0 0.8 dynamic_slice.6.counts
  18.8 0.8 fusion.11
  19.8 1.3 fusion
  21.1 2.1 %copy.30.q_hbm = bf16[512,512]{1,0:T(8,128)(2,1)} copy(bf16[512,512]{0,1:T(8,128)(2,1)} %fusion) | data formatting | bytes 1048576 | tf_op jit(solution)/shard_map/mul | solution.py:527
  23.1 0.5 convolution_convert_fusion
  23.6 1.0 copy.31.g_hbm
  24.6 1.0 copy.28
  25.6 1.0 copy.29
  26.7 0.2 fusion.8
  26.8 0.6 convert_subtract_fusion
  27.4 43.5 %all-to-all-done.x_hbm = bf16[128,32,512]{2,1,0:T(8,128)(2,1)} async-done(((bf16[128,32,512]{2,1,0:T(8,128)(2,1)}), bf16[128,32,512]{2,1,0:T(8,128)(2,1)}, u32[]{:S(2)}, u32[]{:S(2)}) %all-to-all-start) | async-done | bytes 4194336 | tf_op jit(solution)/shard_map/all_to_all | solution.py:497
  70.9 16.6 %forward.1 = (bf16[4096,512]{1,0:T(8,128)(2,1)}, bf16[4096,512]{1,0:T(8,128)(2,1)}, f32[4,8,256]{2,1,0:T(8,128)}, bf16[128,16,128]{2,1,0:T(8,128)(2,1)}) custom-call(s32[128]{0:T(128)} %copy-done.10, s32[4]{0:T(128)} %copy-done.11, bf16[128,32,512]{2,1,0:T(8,128)(2,1)} %all-to-all-done.x_hbm, bf16[512,512]{1,0:T(8,128)(2,1)} %bitcast.22, ...), custom_call_target="tpu_custom_call" | custom-call | flops 10000000000 | bytes 8388608 | tf_op jit(solution)/shard_map/forward/pallas_call | solution.py:344
  87.5 3.7 %all-to-all-start.1 = ((bf16[128,16,128]{2,1,0:T(8,128)(2,1)}), bf16[128,16,128]{2,1,0:T(8,128)(2,1)S(1)}, u32[]{:S(2)}, u32[]{:S(2)}) async-start(bf16[128,16,128]{2,1,0:T(8,128)(2,1)} %get-tuple-element.10), calls=%async_computation.1 | async-start | bytes 1048576 | tf_op jit(solution)/shard_map/all_to_all | solution.py:497
  91.2 22.3 %backward.1 = (bf16[128,144,128]{2,1,0:T(8,128)(2,1)}, bf16[512,512]{1,0:T(8,128)(2,1)}) custom-call(s32[128]{0:T(128)} %copy-done.10, s32[4]{0:T(128)} %copy-done.11, s32[128]{0:T(128)} %get-tuple-element.21.first, s32[128]{0:T(128)} %get-tuple-element.20.last, bf16[4096,512]{1,0:T(8,128)(2,1)} %get-tuple-element.11.k_hbm, ...), custom_call_target="tpu_custom_call" | custom-call | flops 20000000000 | bytes 16777216 | tf_op jit(solution)/shard_map/backward/pallas_call | solution.py:382
  113.5 0.8 copy-done.2
  114.3 2.1 %finish.1 = bf16[128,144,128]{2,1,0:T(8,128)(2,1)} custom-call(bf16[128,16,128]{2,1,0:T(8,128)(2,1)} %copy-done.2, bf16[128,144,128]{2,1,0:T(8,128)(2,1)} %get-tuple-element.14.ret_in), custom_call_target="tpu_custom_call", output_to_operand_aliasing={{}: (1, {})} | custom-call | tf_op jit(solution)/shard_map/finish/pallas_call | solution.py:546
  116.4 10.1 %all-to-all-start.2 = ((bf16[128,144,128]{2,1,0:T(8,128)(2,1)}), bf16[128,144,128]{2,1,0:T(8,128)(2,1)}, u32[]{:S(2)}, u32[]{:S(2)}) async-start(bf16[128,144,128]{2,1,0:T(8,128)(2,1)} %finish.1), calls=%async_computation.2 | async-start | bytes 9437184 | tf_op jit(solution)/shard_map/all_to_all | solution.py:497
  126.7 0.1 reduce_max.19.wanted
  126.8 0.5 fusion.14
  127.3 58.0 %all-to-all-done.2.back_hbm = bf16[128,144,128]{2,1,0:T(8,128)(2,1)} async-done(((bf16[128,144,128]{2,1,0:T(8,128)(2,1)}), bf16[128,144,128]{2,1,0:T(8,128)(2,1)}, u32[]{:S(2)}, u32[]{:S(2)}) %all-to-all-start.2) | async-done | bytes 4718624 | tf_op jit(solution)/shard_map/all_to_all | solution.py:497
  185.3 5.7 %combine.1 = (bf16[16,32,512]{2,1,0:T(8,128)(2,1)}, f32[512,512]{1,0:T(8,128)}) custom-call(s32[128]{0:T(128)S(1)} %reduce_max.19.wanted, bf16[128,144,128]{2,1,0:T(8,128)(2,1)} %all-to-all-done.2.back_hbm, f32[16,32,512]{2,1,0:T(8,128)S(1)} %bitcast.17), custom_call_target="tpu_custom_call" | custom-call | tf_op jit(solution)/shard_map/combine/pallas_call | solution.py:562
  (27 shorter events, 0.3 us)
Async XLA Ops:
  0.6 19.2 %copy-start = (bf16[512,512]{1,0:T(8,128)(2,1)S(1)}, bf16[512,512]{1,0:T(8,128)(2,1)}, u32[]{:S(2)}) copy-start(bf16[512,512]{1,0:T(8,128)(2,1)} %param.10) | copy-start | bytes 1572868
  5.9 13.9 %copy-start.3 = (bf16[1,512,512]{2,1,0:T(8,128)(2,1)S(1)}, bf16[1,512,512]{2,1,0:T(8,128)(2,1)}, u32[]{:S(2)}) copy-start(bf16[1,512,512]{2,1,0:T(8,128)(2,1)} %param.8) | copy-start | bytes 1572868
  5.9 17.2 %copy-start.4 = (bf16[512,512]{1,0:T(8,128)(2,1)S(1)}, bf16[512,512]{1,0:T(8,128)(2,1)}, u32[]{:S(2)}) copy-start(bf16[512,512]{1,0:T(8,128)(2,1)} %param.13) | copy-start | bytes 1572868
  6.0 17.2 %copy-start.5 = (bf16[1,512,512]{2,1,0:T(8,128)(2,1)S(1)}, bf16[1,512,512]{2,1,0:T(8,128)(2,1)}, u32[]{:S(2)}) copy-start(bf16[1,512,512]{2,1,0:T(8,128)(2,1)} %param.9) | copy-start | bytes 1572868
  6.0 64.9 %all-to-all-start = ((bf16[128,32,512]{2,1,0:T(8,128)(2,1)}), bf16[128,32,512]{2,1,0:T(8,128)(2,1)}, u32[]{:S(2)}, u32[]{:S(2)}) async-start(bf16[128,32,512]{2,1,0:T(8,128)(2,1)} %gather.1), calls=%async_computation | async-start | bytes 8388608 | tf_op jit(solution)/shard_map/all_to_all | solution.py:497
  17.9 6.7 %copy-start.6 = (bf16[512,512]{1,0:T(8,128)(2,1)S(1)}, bf16[512,512]{1,0:T(8,128)(2,1)}, u32[]{:S(2)}) copy-start(bf16[512,512]{1,0:T(8,128)(2,1)} %wk_hbm.1) | copy-start | bytes 1572868
  18.0 7.7 %copy-start.7 = (bf16[512,512]{1,0:T(8,128)(2,1)S(1)}, bf16[512,512]{1,0:T(8,128)(2,1)}, u32[]{:S(2)}) copy-start(bf16[512,512]{1,0:T(8,128)(2,1)} %wv_hbm.1) | copy-start | bytes 1572868
  18.8 52.1 %copy-start.11 = (s32[4]{0:T(128)}, s32[4]{0:T(128)S(1)}, u32[]{:S(2)}) copy-start(s32[4]{0:T(128)S(1)} %dynamic_slice.6.counts) | copy-start | bytes 52
  19.8 51.1 %copy-start.10 = (s32[128]{0:T(128)}, s32[128]{0:T(128)S(1)}, u32[]{:S(2)}) copy-start(s32[128]{0:T(128)S(1)} %reshape.27.sources) | copy-start | bytes 1540
  23.6 47.3 %copy-start.1 = (bf16[512,512]{0,1:T(8,128)(2,1)}, bf16[512,512]{0,1:T(8,128)(2,1)S(1)}, u32[]{:S(2)}) copy-start(bf16[512,512]{0,1:T(8,128)(2,1)S(1)} %convolution_convert_fusion) | copy-start | bytes 1572868
  87.5 26.0 %all-to-all-start.1 = ((bf16[128,16,128]{2,1,0:T(8,128)(2,1)}), bf16[128,16,128]{2,1,0:T(8,128)(2,1)S(1)}, u32[]{:S(2)}, u32[]{:S(2)}) async-start(bf16[128,16,128]{2,1,0:T(8,128)(2,1)} %get-tuple-element.10), calls=%async_computation.1 | async-start | bytes 1048576 | tf_op jit(solution)/shard_map/all_to_all | solution.py:497
  113.5 0.8 copy-start.2
  116.4 10.2 %copy-start.9 = (s32[512]{0:T(512)S(1)}, s32[512]{0:T(512)}, u32[]{:S(2)}) copy-start(s32[512]{0:T(512)} %fusion.4.block_max) | copy-start | bytes 6148
  116.4 10.4 %copy-start.8 = (bf16[512,512]{1,0:T(8,128)(2,1)S(1)}, bf16[512,512]{1,0:T(8,128)(2,1)}, u32[]{:S(2)}) copy-start(bf16[512,512]{1,0:T(8,128)(2,1)} %get-tuple-element.15) | copy-start | bytes 1572868
  116.4 68.9 %all-to-all-start.2 = ((bf16[128,144,128]{2,1,0:T(8,128)(2,1)}), bf16[128,144,128]{2,1,0:T(8,128)(2,1)}, u32[]{:S(2)}, u32[]{:S(2)}) async-start(bf16[128,144,128]{2,1,0:T(8,128)(2,1)} %finish.1), calls=%async_computation.2 | async-start | bytes 9437184 | tf_op jit(solution)/shard_map/all_to_all | solution.py:497

commit v5 on v3

--- a/solution.py
+++ b/solution.py
@@ -189,15 +189,15 @@
 def backward_kernel(
     sources, counts, first, last, k_hbm, v_hbm, q_hbm, g_hbm, qt_hbm, gt_hbm, stat_ref, wk_hbm, wv_hbm,
     ret_hbm, dq_ref,
-    ks, vs, ps, ds, dk, dv, acc, q_ref, g_ref, qt_ref, gt_ref, wk_ref, wv_ref, out, sems, wsems, osem,
+    ks, vs, ps, ds, dkv, acc, q_ref, g_ref, qt_ref, gt_ref, w_ref, out, sems, wsems, osem,
 ):
     blocks = q_ref.shape[0] // QUERY_BLOCK
-    width = wk_ref.shape[-1]
+    width = w_ref.shape[-1]
     pairs = width // PAIR
     devices = acc.shape[0]
     weights = [
         (qt_hbm, qt_ref), (gt_hbm, gt_ref), (q_hbm, q_ref), (g_hbm, g_ref),
-        (wk_hbm, wk_ref), (wv_hbm, wv_ref),
+        (wk_hbm, w_ref.at[pl.ds(0, width)]), (wv_hbm, w_ref.at[pl.ds(width, width)]),
     ]
     loads = [pltpu.make_async_copy(a, z, wsems.at[i]) for i, (a, z) in enumerate(weights)]
 
@@ -249,10 +249,10 @@
         gb = split_heads(g_ref[tok, cols])
 
         def do_dv():
-            dv[b % 2, :, cols] = dot(ps[slot], gb).astype(BF16)
+            dkv[b % 2, :, pl.ds(width + p * PAIR, PAIR)] = dot(ps[slot], gb).astype(BF16)
 
         def do_dk():
-            dk[b % 2, :, cols] = dot(ds[slot], qb).astype(BF16)
+            dkv[b % 2, :, cols] = dot(ds[slot], qb).astype(BF16)
 
         def do_dq():
             dq = dot(ks[pl.ds(b * SPAN, SPAN), cols], ds[slot], 0, 0) * F32(HEAD_DIM ** -0.5)
@@ -268,7 +268,7 @@
 
     def back(b, c):
         rows = pl.ds(c * per, per)
-        term = dot(dk[b % 2, rows, :], wk_ref[...]) + dot(dv[b % 2, rows, :], wv_ref[...])
+        term = dot(dkv[b % 2, rows, :], w_ref[...])
         for j in range(segs):
             entry = b * MAXK + c * segs + j
             slot = sources[entry]
@@ -392,15 +392,13 @@
             pltpu.VMEM((blocks * SPAN, width), BF16),
             pltpu.VMEM((2, SPAN, BOTH), BF16),
             pltpu.VMEM((2, SPAN, BOTH), BF16),
-            pltpu.VMEM((2, SPAN, width), BF16),
-            pltpu.VMEM((2, SPAN, width), BF16),
+            pltpu.VMEM((2, SPAN, 2 * width), BF16),
             pltpu.VMEM((devices, KEY_SEG, width), F32),
             pltpu.VMEM((tokens, width), BF16),
             pltpu.VMEM((tokens, width), BF16),
             pltpu.VMEM((width, tokens), BF16),
             pltpu.VMEM((width, tokens), BF16),
-            pltpu.VMEM((width, width), BF16),
-            pltpu.VMEM((width, width), BF16),
+            pltpu.VMEM((2 * width, width), BF16),
             pltpu.VMEM((devices, lines, LANES), BF16),
             pltpu.SemaphoreType.DMA((blocks, 2)),
             pltpu.SemaphoreType.DMA((6,)),
@@ -428,9 +426,8 @@
     pltpu.make_async_copy(out_ref, out_ref, sems.at[1]).wait()
 
 
-def finish_kernel(parts_ref, ret_in, ret_out, wide, sem):
-    total = jnp.sum(parts_ref[...].astype(F32), axis=0)
-    wide[...] = jnp.broadcast_to(total.astype(BF16)[None], wide.shape)
+def finish_kernel(part_ref, ret_in, ret_out, wide, sem):
+    wide[...] = jnp.broadcast_to(part_ref[...][None], wide.shape)
     extra = wide.shape[1]
     rows = pl.ds(ret_out.shape[1] - extra, extra)
     copy = pltpu.make_async_copy(wide, ret_out.at[:, rows], sem)
@@ -438,13 +435,14 @@
     copy.wait()
 
 
-def combine_kernel(wanted, back_hbm, base_ref, out_ref, grad_ref, back, acc, sems):
+def combine_kernel(wanted, back_hbm, base_ref, out_hbm, grad_hbm, back, acc, grad, out, sems, ends):
     devices, lines, _ = back.shape
     groups = sems.shape[0]
     size = devices // groups
     width = base_ref.shape[-1]
     slots = width // LANES
     extra = lines - KEY_SEG * slots
+    tall = size // slots * extra
 
     def copy(t):
         part = pl.ds(t * size, size)
@@ -455,6 +453,12 @@
     acc[...] = base_ref[...]
     for t in range(groups):
         copy(t).wait()
+        for i in range(t * size, (t + 1) * size):
+            rows = pl.ds((i // slots) * extra, extra)
+            cols = pl.ds((i % slots) * LANES, LANES)
+            grad[rows, cols] = back[i, pl.ds(lines - extra, extra), :].astype(F32)
+        part = pl.ds(t * tall, tall)
+        pltpu.make_async_copy(grad.at[part], grad_hbm.at[part], ends.at[0]).start()
 
         def step(i, carry):
             seg = wanted[i]
@@ -468,11 +472,11 @@
             return carry
 
         lax.fori_loop(t * size, (t + 1) * size, step, 0)
-        for i in range(t * size, (t + 1) * size):
-            rows = pl.ds((i // slots) * extra, extra)
-            cols = pl.ds((i % slots) * LANES, LANES)
-            grad_ref[rows, cols] = back[i, pl.ds(lines - extra, extra), :].astype(F32)
-    out_ref[...] = acc[...].astype(out_ref.dtype)
+    out[...] = acc[...].astype(out.dtype)
+    last = pltpu.make_async_copy(out, out_hbm, ends.at[1])
+    last.start()
+    pltpu.make_async_copy(grad, grad_hbm, ends.at[0]).wait()
+    last.wait()
 
 
 def exchange(v):
@@ -526,6 +530,7 @@
         sources, counts, first, last, keys, values, queries, grad_out, queries_t, grad_out_t,
         stats, w_key.T, w_value.T, devices
     )
+    part = jnp.sum(parts.astype(F32), axis=0).astype(BF16)
     ret = pl.pallas_call(
         finish_kernel,
         out_shape=jax.ShapeDtypeStruct(ret.shape, ret.dtype),
@@ -533,8 +538,9 @@
         out_specs=ANY,
         scratch_shapes=[pltpu.VMEM(parts.shape, BF16), pltpu.SemaphoreType.DMA],
         input_output_aliases={1: 0},
+        compiler_params=pltpu.CompilerParams(vmem_limit_bytes=57 * MIB),
         name="finish",
-    )(parts, ret)
+    )(part, ret)
     back = exchange(ret)
     base = dot(dq_t, w_query, 0, 1)
     grad_x, grad_w_out = pl.pallas_call(
@@ -544,11 +550,14 @@
             jax.ShapeDtypeStruct((width, width), F32),
         ],
         in_specs=[SMEM, ANY, VMEM],
-        out_specs=[VMEM, VMEM],
+        out_specs=[ANY, ANY],
         scratch_shapes=[
             pltpu.VMEM(ret.shape, BF16),
             pltpu.VMEM((seg_dev, KEY_SEG, width), F32),
+            pltpu.VMEM((width, width), F32),
+            pltpu.VMEM((seg_dev, KEY_SEG, width), BF16),
             pltpu.SemaphoreType.DMA((8,)),
+            pltpu.SemaphoreType.DMA((2,)),
         ],
         compiler_params=pltpu.CompilerParams(vmem_limit_bytes=24 * MIB),
         name="combine",

time: 191 us -> 190 us (level)
  no operation moved by 1% of the time
where the time goes in v5:
time: 190 us; the launch traced here: 189 us
  waiting for transfers between devices  102 us (54%)
  Pallas kernels  46.4 us (24%)
  starting transfers between devices  27.8 us (15%)
  local copies, waits for them, and re-layouts  6.25 us (3%)
  other arithmetic  3.9 us (2%)
  matrix products  2.22 us (1%)
    all_to_all x3, waiting for transfers between devices, exchange(): return lax.all_to_all(v, AXES, split_axis=0, concat_axis=0, tiled=True)  102 us
    all_to_all x3, starting transfers between devices, exchange(): return lax.all_to_all(v, AXES, split_axis=0, concat_axis=0, tiled=True)  27.8 us
    pallas_call x1, Pallas kernels, backward(): pl.pallas_call(backward_kernel, out_shape=[jax.ShapeDtypeStruct((devices,...  22.3 us
    pallas_call x1, Pallas kernels, forward(): pl.pallas_call(forward_kernel, out_shape=[jax.ShapeDtypeStruct((keys, wid...  14.4 us
    pallas_call x1, Pallas kernels, local(): pl.pallas_call(combine_kernel, out_shape=[jax.ShapeDtypeStruct((seg_dev,...  4.49 us
  transfers between devices with their start and end apart: 3, of which 2 were waited for; matrix products, arithmetic and copies ran while one was open for 5% of the time, Pallas kernels for 12%

profile of v5, /device:TPU:1, one launch (start us, length us, event | category | flops | bytes accessed | tf_op | source)
XLA Modules:
  0.0 189.3 jit_solution(6813364262788400398)
XLA Ops:
  0.7 1.0 fusion.4
  1.7 0.6 reduce_max.18.wanted
  2.4 3.7 %gather.1 = bf16[128,32,512]{2,1,0:T(8,128)(2,1)} custom-call(s32[128]{0:T(128)} %reduce_max.18.wanted, bf16[16,32,512]{2,1,0:T(8,128)(2,1)} %bitcast.20), custom_call_target="tpu_custom_call" | custom-call | tf_op jit(solution)/shard_map/gather/pallas_call | solution.py:501
  6.1 12.0 %all-to-all-start = ((bf16[128,32,512]{2,1,0:T(8,128)(2,1)}), bf16[128,32,512]{2,1,0:T(8,128)(2,1)}, u32[]{:S(2)}, u32[]{:S(2)}) async-start(bf16[128,32,512]{2,1,0:T(8,128)(2,1)} %gather.1), calls=%async_computation | async-start | bytes 8388608 | tf_op jit(solution)/shard_map/all_to_all | solution.py:483
  18.1 0.8 dynamic_slice.6.counts
  19.0 0.8 fusion.11
  19.9 1.3 fusion
  21.2 2.1 %copy.30.q_hbm = bf16[512,512]{1,0:T(8,128)(2,1)} copy(bf16[512,512]{0,1:T(8,128)(2,1)} %fusion) | data formatting | bytes 1048576 | tf_op jit(solution)/shard_map/mul | solution.py:514
  23.3 0.5 convolution_convert_fusion
  23.8 1.0 copy.31.g_hbm
  24.8 1.0 copy.28
  25.8 1.0 copy.29
  26.8 0.2 fusion.8
  27.0 0.6 convert_subtract_fusion
  27.6 43.5 %all-to-all-done.x_hbm = bf16[128,32,512]{2,1,0:T(8,128)(2,1)} async-done(((bf16[128,32,512]{2,1,0:T(8,128)(2,1)}), bf16[128,32,512]{2,1,0:T(8,128)(2,1)}, u32[]{:S(2)}, u32[]{:S(2)}) %all-to-all-start) | async-done | bytes 4194336 | tf_op jit(solution)/shard_map/all_to_all | solution.py:483
  71.1 14.4 %forward.1 = (bf16[4096,512]{1,0:T(8,128)(2,1)}, bf16[4096,512]{1,0:T(8,128)(2,1)}, f32[4,8,256]{2,1,0:T(8,128)}, bf16[128,16,128]{2,1,0:T(8,128)(2,1)}) custom-call(s32[128]{0:T(128)} %copy-done.9, s32[4]{0:T(128)} %copy-done.10, bf16[128,32,512]{2,1,0:T(8,128)(2,1)} %all-to-all-done.x_hbm, bf16[512,512]{1,0:T(8,128)(2,1)} %bitcast.22, ...), custom_call_target="tpu_custom_call" | custom-call | flops 10000000000 | bytes 8388608 | tf_op jit(solution)/shard_map/forward/pallas_call | solution.py:344
  85.5 5.6 %all-to-all-start.1 = ((bf16[128,16,128]{2,1,0:T(8,128)(2,1)}), bf16[128,16,128]{2,1,0:T(8,128)(2,1)S(1)}, u32[]{:S(2)}, u32[]{:S(2)}) async-start(bf16[128,16,128]{2,1,0:T(8,128)(2,1)} %get-tuple-element.10), calls=%async_computation.1 | async-start | bytes 1048576 | tf_op jit(solution)/shard_map/all_to_all | solution.py:483
  91.0 22.3 %backward.1 = (bf16[128,144,128]{2,1,0:T(8,128)(2,1)}, bf16[512,512]{1,0:T(8,128)(2,1)}) custom-call(s32[128]{0:T(128)} %copy-done.9, s32[4]{0:T(128)} %copy-done.10, s32[128]{0:T(128)} %get-tuple-element.21.first, s32[128]{0:T(128)} %get-tuple-element.20.last, bf16[4096,512]{1,0:T(8,128)(2,1)} %get-tuple-element.11.k_hbm, ...), custom_call_target="tpu_custom_call" | custom-call | flops 20000000000 | bytes 16777216 | tf_op jit(solution)/shard_map/backward/pallas_call | solution.py:382
  113.3 0.7 reduce_sum.12.part_ref
  114.0 1.6 finish.1
  115.6 10.3 %all-to-all-start.2 = ((bf16[128,144,128]{2,1,0:T(8,128)(2,1)}), bf16[128,144,128]{2,1,0:T(8,128)(2,1)}, u32[]{:S(2)}, u32[]{:S(2)}) async-start(bf16[128,144,128]{2,1,0:T(8,128)(2,1)} %finish.1), calls=%async_computation.2 | async-start | bytes 9437184 | tf_op jit(solution)/shard_map/all_to_all | solution.py:483
  126.0 0.5 fusion.14
  126.4 58.2 %all-to-all-done.2.back_hbm = bf16[128,144,128]{2,1,0:T(8,128)(2,1)} async-done(((bf16[128,144,128]{2,1,0:T(8,128)(2,1)}), bf16[128,144,128]{2,1,0:T(8,128)(2,1)}, u32[]{:S(2)}, u32[]{:S(2)}) %all-to-all-start.2) | async-done | bytes 4718624 | tf_op jit(solution)/shard_map/all_to_all | solution.py:483
  184.7 4.5 %combine.1 = (bf16[16,32,512]{2,1,0:T(8,128)(2,1)}, f32[512,512]{1,0:T(8,128)}) custom-call(s32[128]{0:T(128)S(1)} %copy-done.1, bf16[128,144,128]{2,1,0:T(8,128)(2,1)} %all-to-all-done.2.back_hbm, f32[16,32,512]{2,1,0:T(8,128)S(1)} %bitcast.17), custom_call_target="tpu_custom_call" | custom-call | tf_op jit(solution)/shard_map/combine/pallas_call | solution.py:546
  (26 shorter events, 0.3 us)
Async XLA Ops:
  0.6 19.3 %copy-start = (bf16[512,512]{1,0:T(8,128)(2,1)S(1)}, bf16[512,512]{1,0:T(8,128)(2,1)}, u32[]{:S(2)}) copy-start(bf16[512,512]{1,0:T(8,128)(2,1)} %param.10) | copy-start | bytes 1572868
  6.1 13.9 %copy-start.3 = (bf16[1,512,512]{2,1,0:T(8,128)(2,1)S(1)}, bf16[1,512,512]{2,1,0:T(8,128)(2,1)}, u32[]{:S(2)}) copy-start(bf16[1,512,512]{2,1,0:T(8,128)(2,1)} %param.8) | copy-start | bytes 1572868
  6.1 17.2 %copy-start.4 = (bf16[512,512]{1,0:T(8,128)(2,1)S(1)}, bf16[512,512]{1,0:T(8,128)(2,1)}, u32[]{:S(2)}) copy-start(bf16[512,512]{1,0:T(8,128)(2,1)} %param.13) | copy-start | bytes 1572868
  6.1 17.2 %copy-start.5 = (bf16[1,512,512]{2,1,0:T(8,128)(2,1)S(1)}, bf16[1,512,512]{2,1,0:T(8,128)(2,1)}, u32[]{:S(2)}) copy-start(bf16[1,512,512]{2,1,0:T(8,128)(2,1)} %param.9) | copy-start | bytes 1572868
  6.1 64.9 %all-to-all-start = ((bf16[128,32,512]{2,1,0:T(8,128)(2,1)}), bf16[128,32,512]{2,1,0:T(8,128)(2,1)}, u32[]{:S(2)}, u32[]{:S(2)}) async-start(bf16[128,32,512]{2,1,0:T(8,128)(2,1)} %gather.1), calls=%async_computation | async-start | bytes 8388608 | tf_op jit(solution)/shard_map/all_to_all | solution.py:483
  18.1 6.7 %copy-start.6 = (bf16[512,512]{1,0:T(8,128)(2,1)S(1)}, bf16[512,512]{1,0:T(8,128)(2,1)}, u32[]{:S(2)}) copy-start(bf16[512,512]{1,0:T(8,128)(2,1)} %wk_hbm.1) | copy-start | bytes 1572868
  18.1 7.7 %copy-start.7 = (bf16[512,512]{1,0:T(8,128)(2,1)S(1)}, bf16[512,512]{1,0:T(8,128)(2,1)}, u32[]{:S(2)}) copy-start(bf16[512,512]{1,0:T(8,128)(2,1)} %wv_hbm.1) | copy-start | bytes 1572868
  19.0 52.1 %copy-start.10 = (s32[4]{0:T(128)}, s32[4]{0:T(128)S(1)}, u32[]{:S(2)}) copy-start(s32[4]{0:T(128)S(1)} %dynamic_slice.6.counts) | copy-start | bytes 52
  19.9 51.1 %copy-start.9 = (s32[128]{0:T(128)}, s32[128]{0:T(128)S(1)}, u32[]{:S(2)}) copy-start(s32[128]{0:T(128)S(1)} %reshape.25.sources) | copy-start | bytes 1540
  23.8 47.3 %copy-start.2 = (bf16[512,512]{0,1:T(8,128)(2,1)}, bf16[512,512]{0,1:T(8,128)(2,1)S(1)}, u32[]{:S(2)}) copy-start(bf16[512,512]{0,1:T(8,128)(2,1)S(1)} %convolution_convert_fusion) | copy-start | bytes 1572868
  85.5 27.8 %all-to-all-start.1 = ((bf16[128,16,128]{2,1,0:T(8,128)(2,1)}), bf16[128,16,128]{2,1,0:T(8,128)(2,1)S(1)}, u32[]{:S(2)}, u32[]{:S(2)}) async-start(bf16[128,16,128]{2,1,0:T(8,128)(2,1)} %get-tuple-element.10), calls=%async_computation.1 | async-start | bytes 1048576 | tf_op jit(solution)/shard_map/all_to_all | solution.py:483
  115.6 10.3 %copy-start.8 = (bf16[512,512]{1,0:T(8,128)(2,1)S(1)}, bf16[512,512]{1,0:T(8,128)(2,1)}, u32[]{:S(2)}) copy-start(bf16[512,512]{1,0:T(8,128)(2,1)} %get-tuple-element.15) | copy-start | bytes 1572868
  115.6 69.1 %copy-start.1 = (s32[128]{0:T(128)S(1)}, s32[128]{0:T(128)}, u32[]{:S(2)}) copy-start(s32[128]{0:T(128)} %reduce_max.18.wanted) | copy-start | bytes 1540
  115.6 69.0 %all-to-all-start.2 = ((bf16[128,144,128]{2,1,0:T(8,128)(2,1)}), bf16[128,144,128]{2,1,0:T(8,128)(2,1)}, u32[]{:S(2)}, u32[]{:S(2)}) async-start(bf16[128,144,128]{2,1,0:T(8,128)(2,1)} %finish.1), calls=%async_computation.2 | async-start | bytes 9437184 | tf_op jit(solution)/shard_map/all_to_all | solution.py:483

commit v6 on v5

--- a/solution.py
+++ b/solution.py
@@ -189,15 +189,15 @@
 def backward_kernel(
     sources, counts, first, last, k_hbm, v_hbm, q_hbm, g_hbm, qt_hbm, gt_hbm, stat_ref, wk_hbm, wv_hbm,
     ret_hbm, dq_ref,
-    ks, vs, ps, ds, dkv, acc, q_ref, g_ref, qt_ref, gt_ref, w_ref, out, sems, wsems, osem,
+    ks, vs, ps, ds, dk, dv, acc, q_ref, g_ref, qt_ref, gt_ref, wk_ref, wv_ref, out, sems, wsems, osem,
 ):
     blocks = q_ref.shape[0] // QUERY_BLOCK
-    width = w_ref.shape[-1]
+    width = wk_ref.shape[-1]
     pairs = width // PAIR
     devices = acc.shape[0]
     weights = [
         (qt_hbm, qt_ref), (gt_hbm, gt_ref), (q_hbm, q_ref), (g_hbm, g_ref),
-        (wk_hbm, w_ref.at[pl.ds(0, width)]), (wv_hbm, w_ref.at[pl.ds(width, width)]),
+        (wk_hbm, wk_ref), (wv_hbm, wv_ref),
     ]
     loads = [pltpu.make_async_copy(a, z, wsems.at[i]) for i, (a, z) in enumerate(weights)]
 
@@ -249,10 +249,10 @@
         gb = split_heads(g_ref[tok, cols])
 
         def do_dv():
-            dkv[b % 2, :, pl.ds(width + p * PAIR, PAIR)] = dot(ps[slot], gb).astype(BF16)
+            dv[b % 2, :, cols] = dot(ps[slot], gb).astype(BF16)
 
         def do_dk():
-            dkv[b % 2, :, cols] = dot(ds[slot], qb).astype(BF16)
+            dk[b % 2, :, cols] = dot(ds[slot], qb).astype(BF16)
 
         def do_dq():
             dq = dot(ks[pl.ds(b * SPAN, SPAN), cols], ds[slot], 0, 0) * F32(HEAD_DIM ** -0.5)
@@ -268,7 +268,7 @@
 
     def back(b, c):
         rows = pl.ds(c * per, per)
-        term = dot(dkv[b % 2, rows, :], w_ref[...])
+        term = dot(dk[b % 2, rows, :], wk_ref[...]) + dot(dv[b % 2, rows, :], wv_ref[...])
         for j in range(segs):
             entry = b * MAXK + c * segs + j
             slot = sources[entry]
@@ -392,13 +392,15 @@
             pltpu.VMEM((blocks * SPAN, width), BF16),
             pltpu.VMEM((2, SPAN, BOTH), BF16),
             pltpu.VMEM((2, SPAN, BOTH), BF16),
-            pltpu.VMEM((2, SPAN, 2 * width), BF16),
+            pltpu.VMEM((2, SPAN, width), BF16),
+            pltpu.VMEM((2, SPAN, width), BF16),
             pltpu.VMEM((devices, KEY_SEG, width), F32),
             pltpu.VMEM((tokens, width), BF16),
             pltpu.VMEM((tokens, width), BF16),
             pltpu.VMEM((width, tokens), BF16),
             pltpu.VMEM((width, tokens), BF16),
-            pltpu.VMEM((2 * width, width), BF16),
+            pltpu.VMEM((width, width), BF16),
+            pltpu.VMEM((width, width), BF16),
             pltpu.VMEM((devices, lines, LANES), BF16),
             pltpu.SemaphoreType.DMA((blocks, 2)),
             pltpu.SemaphoreType.DMA((6,)),

time: 190 us -> 190 us (level)
  no operation moved by 1% of the time
where the time goes in v6:
time: 190 us; the launch traced here: 189 us
  waiting for transfers between devices  102 us (54%)
  Pallas kernels  46.3 us (24%)
  starting transfers between devices  28.1 us (15%)
  local copies, waits for them, and re-layouts  6.25 us (3%)
  other arithmetic  3.9 us (2%)
  matrix products  2.22 us (1%)
    all_to_all x3, waiting for transfers between devices, exchange(): return lax.all_to_all(v, AXES, split_axis=0, concat_axis=0, tiled=True)  102 us
    all_to_all x3, starting transfers between devices, exchange(): return lax.all_to_all(v, AXES, split_axis=0, concat_axis=0, tiled=True)  28.1 us
    pallas_call x1, Pallas kernels, backward(): pl.pallas_call(backward_kernel, out_shape=[jax.ShapeDtypeStruct((devices,...  22.3 us
    pallas_call x1, Pallas kernels, forward(): pl.pallas_call(forward_kernel, out_shape=[jax.ShapeDtypeStruct((keys, wid...  14.2 us
    pallas_call x1, Pallas kernels, local(): pl.pallas_call(combine_kernel, out_shape=[jax.ShapeDtypeStruct((seg_dev,...  4.52 us
  transfers between devices with their start and end apart: 3, of which 2 were waited for; matrix products, arithmetic and copies ran while one was open for 5% of the time, Pallas kernels for 12%

profile of v6, /device:TPU:1, one launch (start us, length us, event | category | flops | bytes accessed | tf_op | source)
XLA Modules:
  0.0 189.4 jit_solution(8435748678075036585)
XLA Ops:
  0.7 1.0 fusion.4
  1.7 0.6 reduce_max.18.wanted
  2.4 3.7 %gather.1 = bf16[128,32,512]{2,1,0:T(8,128)(2,1)} custom-call(s32[128]{0:T(128)} %reduce_max.18.wanted, bf16[16,32,512]{2,1,0:T(8,128)(2,1)} %bitcast.20), custom_call_target="tpu_custom_call" | custom-call | tf_op jit(solution)/shard_map/gather/pallas_call | solution.py:503
  6.1 12.0 %all-to-all-start = ((bf16[128,32,512]{2,1,0:T(8,128)(2,1)}), bf16[128,32,512]{2,1,0:T(8,128)(2,1)}, u32[]{:S(2)}, u32[]{:S(2)}) async-start(bf16[128,32,512]{2,1,0:T(8,128)(2,1)} %gather.1), calls=%async_computation | async-start | bytes 8388608 | tf_op jit(solution)/shard_map/all_to_all | solution.py:485
  18.1 0.8 dynamic_slice.6.counts
  19.0 0.8 fusion.11
  19.9 1.3 fusion
  21.2 2.1 %copy.30.q_hbm = bf16[512,512]{1,0:T(8,128)(2,1)} copy(bf16[512,512]{0,1:T(8,128)(2,1)} %fusion) | data formatting | bytes 1048576 | tf_op jit(solution)/shard_map/mul | solution.py:516
  23.3 0.5 convolution_convert_fusion
  23.8 1.0 copy.31.g_hbm
  24.8 1.0 copy.28
  25.8 1.0 copy.29
  26.8 0.2 fusion.8
  27.0 0.6 convert_subtract_fusion
  27.6 43.5 %all-to-all-done.x_hbm = bf16[128,32,512]{2,1,0:T(8,128)(2,1)} async-done(((bf16[128,32,512]{2,1,0:T(8,128)(2,1)}), bf16[128,32,512]{2,1,0:T(8,128)(2,1)}, u32[]{:S(2)}, u32[]{:S(2)}) %all-to-all-start) | async-done | bytes 4194336 | tf_op jit(solution)/shard_map/all_to_all | solution.py:485
  71.1 14.2 %forward.1 = (bf16[4096,512]{1,0:T(8,128)(2,1)}, bf16[4096,512]{1,0:T(8,128)(2,1)}, f32[4,8,256]{2,1,0:T(8,128)}, bf16[128,16,128]{2,1,0:T(8,128)(2,1)}) custom-call(s32[128]{0:T(128)} %copy-done.9, s32[4]{0:T(128)} %copy-done.10, bf16[128,32,512]{2,1,0:T(8,128)(2,1)} %all-to-all-done.x_hbm, bf16[512,512]{1,0:T(8,128)(2,1)} %bitcast.22, ...), custom_call_target="tpu_custom_call" | custom-call | flops 10000000000 | bytes 8388608 | tf_op jit(solution)/shard_map/forward/pallas_call | solution.py:344
  85.3 5.8 %all-to-all-start.1 = ((bf16[128,16,128]{2,1,0:T(8,128)(2,1)}), bf16[128,16,128]{2,1,0:T(8,128)(2,1)S(1)}, u32[]{:S(2)}, u32[]{:S(2)}) async-start(bf16[128,16,128]{2,1,0:T(8,128)(2,1)} %get-tuple-element.10), calls=%async_computation.1 | async-start | bytes 1048576 | tf_op jit(solution)/shard_map/all_to_all | solution.py:485
  91.1 22.3 %backward.1 = (bf16[128,144,128]{2,1,0:T(8,128)(2,1)}, bf16[512,512]{1,0:T(8,128)(2,1)}) custom-call(s32[128]{0:T(128)} %copy-done.9, s32[4]{0:T(128)} %copy-done.10, s32[128]{0:T(128)} %get-tuple-element.21.first, s32[128]{0:T(128)} %get-tuple-element.20.last, bf16[4096,512]{1,0:T(8,128)(2,1)} %get-tuple-element.11.k_hbm, ...), custom_call_target="tpu_custom_call" | custom-call | flops 20000000000 | bytes 16777216 | tf_op jit(solution)/shard_map/backward/pallas_call | solution.py:382
  113.4 0.7 reduce_sum.12.part_ref
  114.1 1.6 finish.1
  115.7 10.3 %all-to-all-start.2 = ((bf16[128,144,128]{2,1,0:T(8,128)(2,1)}), bf16[128,144,128]{2,1,0:T(8,128)(2,1)}, u32[]{:S(2)}, u32[]{:S(2)}) async-start(bf16[128,144,128]{2,1,0:T(8,128)(2,1)} %finish.1), calls=%async_computation.2 | async-start | bytes 9437184 | tf_op jit(solution)/shard_map/all_to_all | solution.py:485
  126.0 0.5 fusion.14
  126.5 58.2 %all-to-all-done.2.back_hbm = bf16[128,144,128]{2,1,0:T(8,128)(2,1)} async-done(((bf16[128,144,128]{2,1,0:T(8,128)(2,1)}), bf16[128,144,128]{2,1,0:T(8,128)(2,1)}, u32[]{:S(2)}, u32[]{:S(2)}) %all-to-all-start.2) | async-done | bytes 4718624 | tf_op jit(solution)/shard_map/all_to_all | solution.py:485
  184.8 4.5 %combine.1 = (bf16[16,32,512]{2,1,0:T(8,128)(2,1)}, f32[512,512]{1,0:T(8,128)}) custom-call(s32[128]{0:T(128)S(1)} %copy-done.1, bf16[128,144,128]{2,1,0:T(8,128)(2,1)} %all-to-all-done.2.back_hbm, f32[16,32,512]{2,1,0:T(8,128)S(1)} %bitcast.17), custom_call_target="tpu_custom_call" | custom-call | tf_op jit(solution)/shard_map/combine/pallas_call | solution.py:548
  (26 shorter events, 0.3 us)
Async XLA Ops:
  0.6 19.3 %copy-start = (bf16[512,512]{1,0:T(8,128)(2,1)S(1)}, bf16[512,512]{1,0:T(8,128)(2,1)}, u32[]{:S(2)}) copy-start(bf16[512,512]{1,0:T(8,128)(2,1)} %param.10) | copy-start | bytes 1572868
  6.1 13.9 %copy-start.3 = (bf16[1,512,512]{2,1,0:T(8,128)(2,1)S(1)}, bf16[1,512,512]{2,1,0:T(8,128)(2,1)}, u32[]{:S(2)}) copy-start(bf16[1,512,512]{2,1,0:T(8,128)(2,1)} %param.8) | copy-start | bytes 1572868
  6.1 17.2 %copy-start.4 = (bf16[512,512]{1,0:T(8,128)(2,1)S(1)}, bf16[512,512]{1,0:T(8,128)(2,1)}, u32[]{:S(2)}) copy-start(bf16[512,512]{1,0:T(8,128)(2,1)} %param.13) | copy-start | bytes 1572868
  6.1 17.2 %copy-start.5 = (bf16[1,512,512]{2,1,0:T(8,128)(2,1)S(1)}, bf16[1,512,512]{2,1,0:T(8,128)(2,1)}, u32[]{:S(2)}) copy-start(bf16[1,512,512]{2,1,0:T(8,128)(2,1)} %param.9) | copy-start | bytes 1572868
  6.1 64.9 %all-to-all-start = ((bf16[128,32,512]{2,1,0:T(8,128)(2,1)}), bf16[128,32,512]{2,1,0:T(8,128)(2,1)}, u32[]{:S(2)}, u32[]{:S(2)}) async-start(bf16[128,32,512]{2,1,0:T(8,128)(2,1)} %gather.1), calls=%async_computation | async-start | bytes 8388608 | tf_op jit(solution)/shard_map/all_to_all | solution.py:485
  18.1 6.7 %copy-start.6 = (bf16[512,512]{1,0:T(8,128)(2,1)S(1)}, bf16[512,512]{1,0:T(8,128)(2,1)}, u32[]{:S(2)}) copy-start(bf16[512,512]{1,0:T(8,128)(2,1)} %wk_hbm.1) | copy-start | bytes 1572868
  18.1 7.7 %copy-start.7 = (bf16[512,512]{1,0:T(8,128)(2,1)S(1)}, bf16[512,512]{1,0:T(8,128)(2,1)}, u32[]{:S(2)}) copy-start(bf16[512,512]{1,0:T(8,128)(2,1)} %wv_hbm.1) | copy-start | bytes 1572868
  19.0 52.1 %copy-start.10 = (s32[4]{0:T(128)}, s32[4]{0:T(128)S(1)}, u32[]{:S(2)}) copy-start(s32[4]{0:T(128)S(1)} %dynamic_slice.6.counts) | copy-start | bytes 52
  19.9 51.1 %copy-start.9 = (s32[128]{0:T(128)}, s32[128]{0:T(128)S(1)}, u32[]{:S(2)}) copy-start(s32[128]{0:T(128)S(1)} %reshape.25.sources) | copy-start | bytes 1540
  23.8 47.3 %copy-start.2 = (bf16[512,512]{0,1:T(8,128)(2,1)}, bf16[512,512]{0,1:T(8,128)(2,1)S(1)}, u32[]{:S(2)}) copy-start(bf16[512,512]{0,1:T(8,128)(2,1)S(1)} %convolution_convert_fusion) | copy-start | bytes 1572868
  85.3 28.1 %all-to-all-start.1 = ((bf16[128,16,128]{2,1,0:T(8,128)(2,1)}), bf16[128,16,128]{2,1,0:T(8,128)(2,1)S(1)}, u32[]{:S(2)}, u32[]{:S(2)}) async-start(bf16[128,16,128]{2,1,0:T(8,128)(2,1)} %get-tuple-element.10), calls=%async_computation.1 | async-start | bytes 1048576 | tf_op jit(solution)/shard_map/all_to_all | solution.py:485
  115.7 10.3 %copy-start.8 = (bf16[512,512]{1,0:T(8,128)(2,1)S(1)}, bf16[512,512]{1,0:T(8,128)(2,1)}, u32[]{:S(2)}) copy-start(bf16[512,512]{1,0:T(8,128)(2,1)} %get-tuple-element.15) | copy-start | bytes 1572868
  115.7 69.1 %copy-start.1 = (s32[128]{0:T(128)S(1)}, s32[128]{0:T(128)}, u32[]{:S(2)}) copy-start(s32[128]{0:T(128)} %reduce_max.18.wanted) | copy-start | bytes 1540
  115.7 69.0 %all-to-all-start.2 = ((bf16[128,144,128]{2,1,0:T(8,128)(2,1)}), bf16[128,144,128]{2,1,0:T(8,128)(2,1)}, u32[]{:S(2)}, u32[]{:S(2)}) async-start(bf16[128,144,128]{2,1,0:T(8,128)(2,1)} %finish.1), calls=%async_computation.2 | async-start | bytes 9437184 | tf_op jit(solution)/shard_map/all_to_all | solution.py:485
